TPU v7x, 32 devices: a whole 2x2x4 slice. The times are simulated.
32 devices in a mesh: wave: 8 (over z, x), tile: 4 (over y, core).
Axes of the slice: x: 2, y: 2, z: 4, core: 2. Of those that a mesh axis runs over, the one named last changes fastest.
Arguments:
- scene: float32 [32, 1024, 1024], P('wave', 'tile'), may hold values from -6 to 6
- bank: float32 [32, 8, 8, 128, 128], P('wave', 'tile'), may hold values from -0.046875 to 0.046875
- psf_index: int32 [8, 8, 4], P('tile'), may hold values from 0 to 63, as said below
- psf_weight: int32 [8, 8, 4], P('tile'), may hold values from 1 to 32768
- response: float32 [3, 32], replicated, may hold values from -1 to 1
Outputs:
- colour: float32 [3, 1024, 1024], P(None, ('tile', 'wave'))
Inputs may be any that keep to these rules, and one draw needn't show every extreme that they name: Entry k of tile (r, c) names the field point (psf_index // 8, psf_index % 8), which lies at most one tile row and at most one tile column from (r, c); entry 0 names (r, c) itself.
All inputs are finite; a program needn't handle non-finite values.
Results may differ from a plain program's by a relative error of at most 0.0001.
Values sent between devices are 32-bit elements; how exact they have to be, the bound alone decides.
A program may use at most 64 MiB of HBM per device.

v0:
```python
import math

import jax
import jax.numpy as jnp
from jax import lax
from jax.sharding import PartitionSpec as P

highest = lax.Precision.HIGHEST


def with_halo(cells, sides, width):
    for axis, dim in sides:
        count = lax.axis_size(axis)
        ends = count - 1
        head = lax.slice_in_dim(cells, 0, width, axis=dim)
        tail = lax.slice_in_dim(cells, cells.shape[dim] - width, cells.shape[dim], axis=dim)
        cells = jnp.concatenate(
            [
                lax.ppermute(tail, axis, [(i, (i + 1) % count) for i in range(ends)]),
                cells,
                lax.ppermute(head, axis, [((i + 1) % count, i) for i in range(ends)]),
            ],
            axis=dim,
        )
    return cells


def from_behind(shard, axis, by):
    size = lax.axis_size(axis)
    pairs = [(i, i + by) for i in range(size) if 0 <= i + by < size]
    return lax.ppermute(shard, axis, pairs)


def dft_tables(length):
    counter = lax.iota(jnp.int32, length)
    products = counter[:, None] * counter[None, :] % length
    angles = products.astype(jnp.float32) * (2.0 * math.pi / length)
    return (jnp.cos(angles), jnp.sin(angles))


def forward(blocks, cosine, sine):
    side = blocks.shape[-1]
    cos_top = cosine[:side, :]
    sin_top = sine[:side, :]
    row_real = jnp.einsum("ak,tab->tkb", cos_top, blocks, precision=highest)
    row_imag = -jnp.einsum("ak,tab->tkb", sin_top, blocks, precision=highest)
    spec_real = jnp.einsum("tkb,bl->tkl", row_real, cos_top, precision=highest) + jnp.einsum(
        "tkb,bl->tkl", row_imag, sin_top, precision=highest
    )
    spec_imag = jnp.einsum("tkb,bl->tkl", row_imag, cos_top, precision=highest) - jnp.einsum(
        "tkb,bl->tkl", row_real, sin_top, precision=highest
    )
    return (spec_real, spec_imag)


def inverse(prod_real, prod_imag, cosine, sine):
    length = cosine.shape[0]
    part_real = jnp.einsum("mk,tkl->tml", cosine, prod_real, precision=highest) - jnp.einsum(
        "mk,tkl->tml", sine, prod_imag, precision=highest
    )
    part_imag = jnp.einsum("mk,tkl->tml", sine, prod_real, precision=highest) + jnp.einsum(
        "mk,tkl->tml", cosine, prod_imag, precision=highest
    )
    result = jnp.einsum("tml,ln->tmn", part_real, cosine, precision=highest) - jnp.einsum(
        "tml,ln->tmn", part_imag, sine, precision=highest
    )
    return result / float(length * length)


def blur_row(scene_row, psf_row, cosine, sine):
    tile_cols, side = (psf_row.shape[0], psf_row.shape[-1])
    length = 2 * side
    margin = side // 2
    tile_set = scene_row.reshape(side, tile_cols, side).transpose(1, 0, 2)
    scene_real, scene_imag = forward(tile_set, cosine, sine)
    psf_real, psf_imag = forward(psf_row, cosine, sine)
    prod_real = scene_real * psf_real - scene_imag * psf_imag
    prod_imag = scene_real * psf_imag + scene_imag * psf_real
    circular = inverse(prod_real, prod_imag, cosine, sine)
    left_half = jnp.pad(circular[:, :, :side], ((0, 1), (0, 0), (0, 0)))
    right_half = jnp.pad(circular[:, :, side:], ((1, 0), (0, 0), (0, 0)))
    columns = (left_half + right_half).transpose(1, 0, 2).reshape(length, (tile_cols + 1) * side)
    return columns[:, margin : margin + tile_cols * side]


def blur_wave(scene_plane, extended_plane, mixing, cosine, sine):
    slots, tile_cols, side = (
        extended_plane.shape[0] * extended_plane.shape[1],
        extended_plane.shape[1],
        extended_plane.shape[-1],
    )
    tile_rows = extended_plane.shape[0] - 2
    width = scene_plane.shape[1]
    psf_set = jnp.dot(mixing, extended_plane.reshape(slots, side * side), precision=highest)
    psf_set = psf_set.reshape(tile_rows, tile_cols, side, side)
    scene_rows = scene_plane.reshape(tile_rows, side, width)

    def one_row(inputs):
        return blur_row(inputs[0], inputs[1], cosine, sine)

    rows_out = lax.map(one_row, (scene_rows, psf_set))
    top_half = jnp.pad(rows_out[:, :side], ((0, 1), (0, 0), (0, 0)))
    bottom_half = jnp.pad(rows_out[:, side:], ((1, 0), (0, 0), (0, 0)))
    return (top_half + bottom_half).reshape((tile_rows + 1) * side, width)


def per_device(scene, bank, psf_index, psf_weight, response):
    wave_count, tile_rows, tile_cols, side = (
        bank.shape[0],
        bank.shape[1],
        bank.shape[2],
        bank.shape[3],
    )
    entries = psf_index.shape[-1]
    margin = side // 2
    strip = tile_rows * side
    extended = with_halo(bank, (("tile", 1),), 1)
    first_slot = (lax.axis_index("tile") * tile_rows - 1) * tile_cols
    local_slot = psf_index.reshape(tile_rows * tile_cols, entries) - first_slot
    slot_ids = lax.iota(jnp.int32, (tile_rows + 2) * tile_cols)
    fraction = psf_weight.reshape(tile_rows * tile_cols, entries).astype(jnp.float32) / 65536.0
    mixing = jnp.sum(
        jnp.where(local_slot[:, :, None] == slot_ids[None, None, :], fraction[:, :, None], 0.0),
        axis=1,
    )
    cosine, sine = dft_tables(2 * side)

    def one_wave(inputs):
        return blur_wave(inputs[0], inputs[1], mixing, cosine, sine)

    summed = lax.map(one_wave, (scene, extended))
    from_above = from_behind(summed[:, strip + margin :], "tile", 1)
    from_below = from_behind(summed[:, :margin], "tile", -1)
    blurred = summed[:, margin : margin + strip]
    blurred = blurred.at[:, :margin].add(from_above)
    blurred = blurred.at[:, strip - margin :].add(from_below)
    own_response = lax.dynamic_slice_in_dim(
        response, lax.axis_index("wave") * wave_count, wave_count, 1
    )
    partial_sums = jnp.einsum("cw,wrx->crx", own_response, blurred, precision=highest)
    colour = lax.psum_scatter(partial_sums, "wave", scatter_dimension=1, tiled=True)
    return colour


def solution(mesh):
    in_specs = (
        P("wave", "tile", None),
        P("wave", "tile", None, None, None),
        P("tile", None, None),
        P("tile", None, None),
        P(),
    )
    out_specs = P(None, ("tile", "wave"), None)
    return jax.shard_map(
        per_device, mesh=mesh, in_specs=in_specs, out_specs=out_specs, check_vma=False
    )
```

profile of v0, /device:TPU:4, one launch (start us, length us, event | category | flops | bytes accessed | tf_op | source)
XLA Modules:
  0.0 683.2 jit_solution(4985707934514981831)
XLA Ops:
  6.5 4.0 fusion.78
  12.4 3.6 collective-permute-start.1
  16.4 21.8 %collective-permute-done = f32[4,1,8,128,128]{4,3,2,1,0:T(8,128)} collective-permute-done((f32[4,1,8,128,128]{4,3,2,1,0:T(8,128)}, f32[4,1,8,128,128]{4,3,2,1,0:T(8,128)}, u32[]{:S(2)}, u32[]{:S(2)}) %collective-permute-start) | collective-permute-done | bytes 2097184 | tf_op jit(solution)/shard_map/ppermute | solution.py:19
  39.6 5.9 pad_maximum_fusion
  45.5 419.0 %while.42 = (s32[]{:T(128)}, f32[4,384,1024]{2,1,0:T(8,128)}, f32[4,256,1024]{2,1,0:T(8,128)}, f32[4,4,8,128,128]{4,3,2,1,0:T(8,128)}, f32[16,32]{1,0:T(8,128)S(1)}, /*index=5*/s32[]{:T(128)}, s32[]{:T(128)}, s32[]{:T(128)}) while((s32[]{:T(128)}, f32[4,384,1024]{2,1,0:T(8,128)}, f32[4,256,1024]{2,1,0:T(8,128)}, ...), condition=%wide.region_4.5_spmd.clone.clone, body=%wide.region_1.4_spmd.clone.clone.sunk | while | flops 17826873344 | bytes 141692272 | solution.py:131
  53.0 92.2 %while.43 = (s32[]{:T(128)}, f32[2,256,1024]{1,2,0:T(8,128)}, f32[2,128,1024]{2,1,0:T(8,128)S(1)}, f32[256,256]{1,0:T(8,128)S(1)}, f32[256,256]{1,0:T(8,128)S(1)}, /*index=5*/f32[2,8,128,128]{3,1,2,0:T(8,128)}, s32[]{:T(128)}) while((s32[]{:T(128)}, f32[2,256,1024]{1,2,0:T(8,128)}, f32[2,128,1024]{2,1,0:T(8,128)S(1)}, ...), condition=%wide.region_3.3_spmd.clone, body=%wide.region_2.2_spmd.clone.sunk | while | flops 17724899328 | bytes 117572296 | solution.py:101
  77.9 3.6 fusion.193
  81.5 3.8 fusion.194
  87.4 3.6 fusion.196
  123.0 3.6 fusion.193
  126.6 4.0 fusion.194
  156.4 92.1 %while.43 = (s32[]{:T(128)}, f32[2,256,1024]{1,2,0:T(8,128)}, f32[2,128,1024]{2,1,0:T(8,128)S(1)}, f32[256,256]{1,0:T(8,128)S(1)}, f32[256,256]{1,0:T(8,128)S(1)}, /*index=5*/f32[2,8,128,128]{3,1,2,0:T(8,128)}, s32[]{:T(128)}) while((s32[]{:T(128)}, f32[2,256,1024]{1,2,0:T(8,128)}, f32[2,128,1024]{2,1,0:T(8,128)S(1)}, ...), condition=%wide.region_3.3_spmd.clone, body=%wide.region_2.2_spmd.clone.sunk | while | flops 17724899328 | bytes 117572296 | solution.py:101
  181.3 3.6 fusion.193
  184.9 3.8 fusion.194
  226.4 3.6 fusion.193
  230.0 4.0 fusion.194
  259.7 92.1 %while.43 = (s32[]{:T(128)}, f32[2,256,1024]{1,2,0:T(8,128)}, f32[2,128,1024]{2,1,0:T(8,128)S(1)}, f32[256,256]{1,0:T(8,128)S(1)}, f32[256,256]{1,0:T(8,128)S(1)}, /*index=5*/f32[2,8,128,128]{3,1,2,0:T(8,128)}, s32[]{:T(128)}) while((s32[]{:T(128)}, f32[2,256,1024]{1,2,0:T(8,128)}, f32[2,128,1024]{2,1,0:T(8,128)S(1)}, ...), condition=%wide.region_3.3_spmd.clone, body=%wide.region_2.2_spmd.clone.sunk | while | flops 17724899328 | bytes 117572296 | solution.py:101
  284.6 3.6 fusion.193
  288.2 3.8 fusion.194
  294.1 3.6 fusion.196
  329.7 3.6 fusion.193
  333.3 4.0 fusion.194
  363.1 92.1 %while.43 = (s32[]{:T(128)}, f32[2,256,1024]{1,2,0:T(8,128)}, f32[2,128,1024]{2,1,0:T(8,128)S(1)}, f32[256,256]{1,0:T(8,128)S(1)}, f32[256,256]{1,0:T(8,128)S(1)}, /*index=5*/f32[2,8,128,128]{3,1,2,0:T(8,128)}, s32[]{:T(128)}) while((s32[]{:T(128)}, f32[2,256,1024]{1,2,0:T(8,128)}, f32[2,128,1024]{2,1,0:T(8,128)S(1)}, ...), condition=%wide.region_3.3_spmd.clone, body=%wide.region_2.2_spmd.clone.sunk | while | flops 17724899328 | bytes 117572296 | solution.py:101
  388.0 3.6 fusion.193
  391.6 3.8 fusion.194
  433.1 3.6 fusion.193
  436.7 4.0 fusion.194
  467.8 4.7 slice.132
  472.5 9.7 %collective-permute-done.2 = f32[4,64,1024]{2,1,0:T(8,128)S(1)} collective-permute-done((f32[4,64,1024]{2,1,0:T(8,128)S(1)}, f32[4,64,1024]{2,1,0:T(8,128)S(1)}, u32[]{:S(2)}, u32[]{:S(2)}) %collective-permute-start.2) | collective-permute-done | bytes 1048608 | tf_op jit(solution)/shard_map/ppermute | solution.py:31
  487.0 12.3 %collective-permute-done.3 = f32[4,64,1024]{2,1,0:T(8,128)S(1)} collective-permute-done((f32[4,64,1024]{2,1,0:T(8,128)S(1)}, f32[4,64,1024]{2,1,0:T(8,128)S(1)}, u32[]{:S(2)}, u32[]{:S(2)}) %collective-permute-start.3) | collective-permute-done | bytes 1048608 | tf_op jit(solution)/shard_map/ppermute | solution.py:31
  501.7 14.0 %fusion.69 = f32[3,256,1024]{2,0,1:T(4,128)} fusion(f32[4,256,1024]{2,1,0:T(8,128)} %fusion.71, f32[3,32]{1,0:T(4,128)S(1)} %copy-done, s32[]{:T(128)S(6)} %select_n.48), kind=kOutput, calls=%fused_computation.86 | convolution fusion | flops 37748736 | bytes 7340420 | tf_op jit(solution)/shard_map/cw,wrx->crx/dot_general | solution.py:140
  517.6 156.3 %all-reduce.7.cloned.1.call-done = f32[3,256,1024]{2,0,1:T(4,128)} async-done(((f32[3,256,1024]{2,0,1:T(4,128)}), f32[3,256,1024]{2,0,1:T(4,128)}) %all-reduce.7.cloned.1.call-update) | async-done | bytes 3145744
  (310 shorter events, 352.8 us)
Async XLA Ops:
  6.5 495.2 %copy-start = (f32[3,32]{1,0:T(4,128)S(1)}, f32[3,32]{1,0:T(4,128)}, u32[]{:S(2)}) copy-start(f32[3,32]{1,0:T(4,128)} %param.17) | copy-start | bytes 1156
  6.5 9.6 %copy-start.5 = (s32[2,8,4]{1,2,0:T(4,128)S(1)}, s32[2,8,4]{1,2,0:T(4,128)}, u32[]{:S(2)}) copy-start(s32[2,8,4]{1,2,0:T(4,128)} %param.15) | copy-start | bytes 772
  6.5 9.7 %copy-start.6 = (s32[2,8,4]{1,2,0:T(4,128)S(1)}, s32[2,8,4]{1,2,0:T(4,128)}, u32[]{:S(2)}) copy-start(s32[2,8,4]{1,2,0:T(4,128)} %param.16) | copy-start | bytes 772
  6.5 667.3 %all-reduce.7.cloned.1.call-start = ((), (), s32[]{:S(2)}) async-start(), calls=%async_computation | async-start | bytes 8388608
  10.5 27.7 %collective-permute-start = (f32[4,1,8,128,128]{4,3,2,1,0:T(8,128)}, f32[4,1,8,128,128]{4,3,2,1,0:T(8,128)}, u32[]{:S(2)}, u32[]{:S(2)}) collective-permute-start(f32[4,1,8,128,128]{4,3,2,1,0:T(8,128)} %get-tuple-element.463), channel_id=1, source_target_pairs={{0,1},{1,2},{2,3},{4,5},{5,6},{6,7},{8,9},{9,10},{10,11},{12,13},{... | collective-permute-start | bytes 6291464 | tf_op jit(solution)/shard_map/ppermute | solution.py:19
  12.4 27.2 %collective-permute-start.1 = (f32[4,1,8,128,128]{4,3,2,1,0:T(8,128)S(1)}, f32[4,1,8,128,128]{4,3,2,1,0:T(8,128)}, u32[]{:S(2)}, u32[]{:S(2)}) collective-permute-start(f32[4,1,8,128,128]{4,3,2,1,0:T(8,128)S(1)} %get-tuple-element.464), channel_id=1, source_target_pairs={{1,0},{2,1},{3,2},{5,4},{6,5},{7,6},{9,8},{10,9},{11,10},{13,12},{... | collective-permute-start | bytes 6291464 | tf_op jit(solution)/shard_map/ppermute | solution.py:21
  58.2 3.2 copy-start.2
  73.5 1.9 copy-start.1
  97.0 1.3 copy-start.4
  103.6 3.2 copy-start.2
  118.6 1.9 copy-start.1
  142.4 1.3 copy-start.4
  161.5 3.2 copy-start.2
  176.8 1.9 copy-start.1
  200.4 1.3 copy-start.4
  206.9 3.2 copy-start.2
  222.0 1.9 copy-start.1
  245.8 1.3 copy-start.4
  264.8 3.2 copy-start.2
  280.2 1.9 copy-start.1
  303.7 1.3 copy-start.4
  310.2 3.2 copy-start.2
  325.3 1.9 copy-start.1
  349.1 1.3 copy-start.4
  368.2 3.2 copy-start.2
  383.6 1.9 copy-start.1
  407.1 1.3 copy-start.4
  413.7 3.2 copy-start.2
  428.7 1.9 copy-start.1
  452.5 1.3 copy-start.4
  465.8 16.4 %collective-permute-start.2 = (f32[4,64,1024]{2,1,0:T(8,128)S(1)}, f32[4,64,1024]{2,1,0:T(8,128)S(1)}, u32[]{:S(2)}, u32[]{:S(2)}) collective-permute-start(f32[4,64,1024]{2,1,0:T(8,128)S(1)} %slice.134), channel_id=1, source_target_pairs={{0,1},{1,2},{2,3},{4,5},{5,6},{6,7},{8,9},{9,10},{10,11},{12,13},{... | collective-permute-start | bytes 3145736 | tf_op jit(solution)/shard_map/ppermute | solution.py:31
  485.1 14.2 %collective-permute-start.3 = (f32[4,64,1024]{2,1,0:T(8,128)S(1)}, f32[4,64,1024]{2,1,0:T(8,128)S(1)}, u32[]{:S(2)}, u32[]{:S(2)}) collective-permute-start(f32[4,64,1024]{2,1,0:T(8,128)S(1)} %get-tuple-element.461), channel_id=1, source_target_pairs={{1,0},{2,1},{3,2},{5,4},{6,5},{7,6},{9,8},{10,9},{11,10},{13,12},{... | collective-permute-start | bytes 3145736 | tf_op jit(solution)/shard_map/ppermute | solution.py:31
  (9 other events, 8.8 us)
Sparse Core Ops, SparseCore 0:
  515.9 157.9 all-reduce.6
where the time goes:
time: 688 us; the launch traced here: 683 us
  matrix products  350 us (51%)
  waiting for transfers between devices  202 us (29%)
  local copies, waits for them, and re-layouts  74.2 us (11%)
  other arithmetic  17.4 us (3%)
  loops' own time  16.7 us (2%)
  between operations  14.5 us (2%)
  starting transfers between devices  9.38 us (1%)
    unnamed x2, waiting for transfers between devices  156 us
    dot_general x16, matrix products, forward(): jnp.einsum('tkb,bl->tkl', row_imag, sin_top, precision=highest)  41.1 us
    dot_general x16, matrix products, forward(): jnp.einsum('tkb,bl->tkl', row_real, sin_top, precision=highest)  35.3 us
    dot_general x16, matrix products, forward(): jnp.einsum('tkb,bl->tkl', row_real, cos_top, precision=highest)  32.5 us
    dot_general x8, matrix products, inverse(): jnp.einsum('mk,tkl->tml', cosine, prod_imag, precision=highest)  31 us
    dot_general x16, matrix products, forward(): jnp.einsum('tkb,bl->tkl', row_imag, cos_top, precision=highest)  30 us
    dot_general x8, matrix products, inverse(): jnp.einsum('mk,tkl->tml', sine, prod_real, precision=highest)  28.7 us
    dot_general x8, matrix products, inverse(): jnp.einsum('mk,tkl->tml', cosine, prod_real, precision=highest)  28.7 us
  transfers between devices with their start and end apart: 5, of which 5 were waited for; matrix products, arithmetic and copies ran while one was open for 1% of the time, Pallas kernels for 0%

commit v1 on v0

v1 whole, which is shorter than its diff:
```python
import functools

import jax
import jax.numpy as jnp
import ml_dtypes
import numpy as np
from jax import lax
from jax.experimental import pallas as pl
from jax.experimental.pallas import tpu as pltpu
from jax.sharding import PartitionSpec as P

CHUNKS = 2
CHUNK_ROWS = 16
VMEM_BYTES = 56 * 1024 * 1024


def halves(table):
    high = table.astype(ml_dtypes.bfloat16)
    low = (table - high.astype(np.float64)).astype(ml_dtypes.bfloat16)
    return high, low


def left_factor(table):
    high, low = halves(table)
    return np.concatenate([high, high, low], axis=1)


def right_factor(table):
    high, low = halves(table)
    return np.concatenate([high, high, low], axis=0)


def tables(side):
    length = 2 * side
    odd = 2 * np.arange(side)[:, None] + 1
    angle = np.pi * (odd * np.arange(length)[None, :] % (2 * length)) / length
    cosine, sine = np.cos(angle), np.sin(angle)
    rows_in = np.concatenate([cosine[:, :side], -sine[:, :side]], axis=0)
    cols_in = np.concatenate([cosine[:, :side].T, sine[:, :side].T], axis=1)
    cols_out = np.concatenate([cosine, sine], axis=0)
    rows_out = np.concatenate([cosine.T, -sine.T], axis=1) * (2.0 / (length * length))
    return left_factor(rows_in), right_factor(cols_in), right_factor(cols_out), left_factor(rows_out)


def split(values):
    high = values.astype(jnp.bfloat16)
    low = (values - high.astype(jnp.float32)).astype(jnp.bfloat16)
    return high, low


def dot(left, right):
    return jnp.dot(left, right, preferred_element_type=jnp.float32)


def put_rows(out_ref, values, side, lanes):
    high, low = split(values)
    out_ref[0:side, lanes] = high
    out_ref[side : 2 * side, lanes] = low
    out_ref[2 * side : 3 * side, lanes] = high


def put_cols(out_ref, values, width, rows):
    high, low = split(values)
    out_ref[rows, 0:width] = high
    out_ref[rows, width : 2 * width] = low
    out_ref[rows, 2 * width : 3 * width] = high


def scene_kernel(side, tile_cols, rows_ref, cols_ref, scene_ref, out_ref, lifted, mid, spec):
    put_rows(lifted, scene_ref[0], side, slice(None))
    first = dot(rows_ref[...], lifted[...])
    for c in range(tile_cols):
        put_cols(mid, first[:, c * side : (c + 1) * side], side, slice(2 * c * side, 2 * (c + 1) * side))
    spec[...] = dot(mid[...], cols_ref[...])
    for c in range(tile_cols):
        top = 2 * c * side
        a = spec[top : top + side, 0:side]
        b = spec[top : top + side, side : 2 * side]
        d = spec[top + side : top + 2 * side, 0:side]
        e = spec[top + side : top + 2 * side, side : 2 * side]
        out_ref[0, 0, c, 0:side, 0:side] = a + e
        out_ref[0, 0, c, side : 2 * side, 0:side] = d - b
        out_ref[0, 0, c, 0:side, side : 2 * side] = a - e
        out_ref[0, 0, c, side : 2 * side, side : 2 * side] = d + b


def scene_spectra(scene, row_table, col_table, side):
    waves, strip, width = scene.shape
    tile_rows, tile_cols = strip // side, width // side
    whole = lambda w, r: (0, 0)
    return pl.pallas_call(
        functools.partial(scene_kernel, side, tile_cols),
        grid=(waves, tile_rows),
        in_specs=[
            pl.BlockSpec(row_table.shape, whole),
            pl.BlockSpec(col_table.shape, whole),
            pl.BlockSpec((1, side, width), lambda w, r: (w, r, 0)),
        ],
        out_specs=pl.BlockSpec((1, 1, tile_cols, 2 * side, 2 * side), lambda w, r: (w, r, 0, 0, 0)),
        out_shape=jax.ShapeDtypeStruct((waves, tile_rows, tile_cols, 2 * side, 2 * side), jnp.float32),
        scratch_shapes=[
            pltpu.VMEM((3 * side, width), jnp.bfloat16),
            pltpu.VMEM((2 * side * tile_cols, 3 * side), jnp.bfloat16),
            pltpu.VMEM((2 * side * tile_cols, 2 * side), jnp.float32),
        ],
        compiler_params=pltpu.CompilerParams(vmem_limit_bytes=VMEM_BYTES),
        cost_estimate=pl.CostEstimate(
            flops=waves * tile_rows * tile_cols * 12 * 2 * side**3,
            bytes_accessed=5 * 4 * waves * strip * width,
            transcendentals=0,
        ),
        name="scene_spectra",
    )(row_table, col_table, scene)


def colour_kernel(
    dims,
    slot_ref,
    weight_ref,
    response_ref,
    rows_in,
    cols_in,
    cols_out,
    rows_out,
    spec_ref,
    own_ref,
    above_ref,
    below_ref,
    carry_in,
    out_ref,
    carry_out,
    extended,
    carry,
    psf_lifted,
    psf_mid,
    psf_spec,
    mixed,
    back,
    copied,
):
    first_col, count, tile_rows, tile_cols, entries, side, waves, channels = dims
    step = pl.program_id(0)
    length = 2 * side

    @pl.when(step == 0)
    def _():
        inner = tile_rows * tile_cols
        copies = [
            pltpu.make_async_copy(above_ref, extended.at[:, pl.ds(0, tile_cols)], copied.at[0]),
            pltpu.make_async_copy(own_ref, extended.at[:, pl.ds(tile_cols, inner)], copied.at[1]),
            pltpu.make_async_copy(below_ref, extended.at[:, pl.ds(tile_cols + inner, tile_cols)], copied.at[2]),
        ]
        for copy in copies:
            copy.start()
        carry[...] = carry_in[...]
        for copy in copies:
            copy.wait()

    @pl.when(step < count)
    def _():
        for r in range(tile_rows):
            place = (r * tile_cols + first_col + step) * entries
            for w in range(waves):
                psf = weight_ref[place] * extended[w, slot_ref[place]]
                for k in range(1, entries):
                    psf = psf + weight_ref[place + k] * extended[w, slot_ref[place + k]]
                put_rows(psf_lifted, psf, side, slice(w * side, (w + 1) * side))
            first = dot(rows_in[...], psf_lifted[...])
            for w in range(waves):
                put_cols(
                    psf_mid, first[:, w * side : (w + 1) * side], side, slice(w * length, (w + 1) * length)
                )
            psf_spec[...] = dot(psf_mid[...], cols_in[...])

            def some_rows(index, state):
                start = pl.multiple_of(index * CHUNK_ROWS, CHUNK_ROWS)
                upper = pl.ds(start, CHUNK_ROWS)
                lower = pl.ds(start + side, CHUNK_ROWS)
                left, right = slice(0, side), slice(side, length)
                sums = [None] * channels
                for w in range(waves):
                    p_upper = pl.ds(start + w * length, CHUNK_ROWS)
                    p_lower = pl.ds(start + w * length + side, CHUNK_ROWS)
                    a, b = psf_spec[p_upper, left], psf_spec[p_upper, right]
                    d, e = psf_spec[p_lower, left], psf_spec[p_lower, right]
                    p1r, p1i, p2r, p2i = a + e, d - b, a - e, d + b
                    s1r, s1i = spec_ref[w, r, 0, upper, left], spec_ref[w, r, 0, lower, left]
                    s2r, s2i = spec_ref[w, r, 0, upper, right], spec_ref[w, r, 0, lower, right]
                    q1r, q1i = s1r * p1r - s1i * p1i, s1r * p1i + s1i * p1r
                    q2r, q2i = s2r * p2r - s2i * p2i, s2r * p2i + s2i * p2r
                    parts = (q1r + q2r, q2i - q1i, q1i + q2i, q1r - q2r)
                    for ch in range(channels):
                        gain = response_ref[ch, w]
                        terms = [gain * part for part in parts]
                        sums[ch] = terms if w == 0 else [old + new for old, new in zip(sums[ch], terms)]
                for ch in range(channels):
                    for j, rows in ((0, pl.ds(start + ch * length, CHUNK_ROWS)), (2, pl.ds(start + ch * length + side, CHUNK_ROWS))):
                        for h in range(2):
                            high, low = split(sums[ch][j + h])
                            mixed[rows, h * side : (h + 1) * side] = high
                            mixed[rows, length + h * side : length + (h + 1) * side] = low
                            mixed[rows, 2 * length + h * side : 2 * length + (h + 1) * side] = high
                return state

            lax.fori_loop(0, side // CHUNK_ROWS, some_rows, 0)
            partial = dot(mixed[...], cols_out[...])
            for ch in range(channels):
                rows = slice(ch * length, (ch + 1) * length)
                lane = (r * channels + ch) * side
                block = partial[rows, 0:side] + carry[r, rows, :]
                put_rows(back, block, length, slice(lane, lane + side))
                carry[r, rows, :] = partial[rows, side:length]

    @pl.when(step >= count)
    def _():
        for r in range(tile_rows):
            for ch in range(channels):
                rows = slice(ch * length, (ch + 1) * length)
                lane = (r * channels + ch) * side
                put_rows(back, carry[r, rows, :], length, slice(lane, lane + side))

    light = dot(rows_out[...], back[...])
    for ch in range(channels):
        for r in range(tile_rows + 1):
            total = None
            if r < tile_rows:
                lane = (r * channels + ch) * side
                total = light[0:side, lane : lane + side]
            if r > 0:
                lane = ((r - 1) * channels + ch) * side
                low = light[side:length, lane : lane + side]
                total = low if total is None else total + low
            out_ref[ch, r * side : (r + 1) * side, :] = total

    @pl.when(step == pl.num_programs(0) - 1)
    def _():
        carry_out[...] = carry[...]


def colour_columns(spectra, own, above, below, slots, weights, response, carry, cols, side):
    row_in, col_in, col_out, row_out = tables(side)
    waves, tile_rows, tile_cols = spectra.shape[:3]
    channels = response.shape[0]
    length = 2 * side
    first_col, count = cols
    entries = slots.shape[0] // (tile_rows * tile_cols)
    steps = count + (1 if first_col + count == tile_cols else 0)
    dims = (first_col, count, tile_rows, tile_cols, entries, side, waves, channels)
    smem = pl.BlockSpec(memory_space=pltpu.SMEM)
    anywhere = pl.BlockSpec(memory_space=pl.ANY)
    whole = lambda c: (0, 0)
    return pl.pallas_call(
        functools.partial(colour_kernel, dims),
        grid=(steps,),
        in_specs=[
            smem,
            smem,
            smem,
            pl.BlockSpec(row_in.shape, whole),
            pl.BlockSpec(col_in.shape, whole),
            pl.BlockSpec(col_out.shape, whole),
            pl.BlockSpec(row_out.shape, whole),
            pl.BlockSpec(
                (waves, tile_rows, 1, length, length),
                lambda c: (0, 0, first_col + jnp.minimum(c, count - 1), 0, 0),
            ),
            anywhere,
            anywhere,
            anywhere,
            pl.BlockSpec(carry.shape, lambda c: (0, 0, 0)),
        ],
        out_specs=[
            pl.BlockSpec((channels, (tile_rows + 1) * side, side), lambda c: (0, 0, c)),
            pl.BlockSpec(carry.shape, lambda c: (0, 0, 0)),
        ],
        out_shape=[
            jax.ShapeDtypeStruct((channels, (tile_rows + 1) * side, steps * side), jnp.float32),
            jax.ShapeDtypeStruct(carry.shape, jnp.float32),
        ],
        scratch_shapes=[
            pltpu.VMEM((waves, (tile_rows + 2) * tile_cols, side, side), jnp.float32),
            pltpu.VMEM(carry.shape, jnp.float32),
            pltpu.VMEM((3 * side, waves * side), jnp.bfloat16),
            pltpu.VMEM((waves * length, 3 * side), jnp.bfloat16),
            pltpu.VMEM((waves * length, length), jnp.float32),
            pltpu.VMEM((channels * length, 3 * length), jnp.bfloat16),
            pltpu.VMEM((3 * length, tile_rows * channels * side), jnp.bfloat16),
            pltpu.SemaphoreType.DMA((3,)),
        ],
        compiler_params=pltpu.CompilerParams(vmem_limit_bytes=VMEM_BYTES),
        cost_estimate=pl.CostEstimate(
            flops=count * tile_rows * (waves * 12 + channels * 36) * 2 * side**3,
            bytes_accessed=4 * waves * tile_rows * count * length * length,
            transcendentals=0,
        ),
        name="colour_columns",
    )(slots, weights, response, row_in, col_in, col_out, row_out, spectra, own, above, below, carry)


def shifted(values, axis, by):
    size = lax.axis_size(axis)
    return lax.ppermute(values, axis, [(i, i + by) for i in range(size) if 0 <= i + by < size])


def scatter_sum(values, axis, x_first):
    size = lax.axis_size(axis)
    bits = size.bit_length() - 1
    channels, rows, columns = values.shape
    me = lax.axis_index(axis)
    values = values.reshape((channels,) + (2,) * bits + (rows // size, columns))
    left = list(range(bits - 1, -1, -1))
    order = list(range(bits)) if x_first else list(range(1, bits)) + [0]
    for bit in order:
        dim = 1 + left.index(bit)
        mine = (me >> bit) & 1
        keep = lax.dynamic_index_in_dim(values, mine, dim, keepdims=False)
        give = lax.dynamic_index_in_dim(values, 1 - mine, dim, keepdims=False)
        values = keep + lax.ppermute(give, axis, [(i, i ^ (1 << bit)) for i in range(size)])
        left.remove(bit)
    return values


def per_device(scene, bank, psf_index, psf_weight, response):
    waves, tile_rows, tile_cols, side = bank.shape[:4]
    entries = psf_index.shape[-1]
    margin = side // 2
    strip = tile_rows * side
    channels = response.shape[0]
    above = shifted(bank[:, tile_rows - 1], "tile", 1)
    below = shifted(bank[:, 0], "tile", -1)
    own = bank.reshape(waves, tile_rows * tile_cols, side, side)
    first_slot = (lax.axis_index("tile") * tile_rows - 1) * tile_cols
    slots = (psf_index - first_slot).reshape(tile_rows * tile_cols * entries)
    weights = (psf_weight.astype(jnp.float32) / 65536.0).reshape(tile_rows * tile_cols * entries)
    own_response = lax.dynamic_slice_in_dim(response, lax.axis_index("wave") * waves, waves, 1)
    row_in, col_in, _, _ = tables(side)
    spectra = scene_spectra(scene, row_in, col_in, side)
    carry = jnp.zeros((tile_rows, channels * 2 * side, side), jnp.float32)
    count = tile_cols // CHUNKS
    pieces = []
    for g in range(CHUNKS):
        light, carry = colour_columns(
            spectra, own, above, below, slots, weights, own_response, carry, (g * count, count), side
        )
        from_above = shifted(light[:, strip + margin :], "tile", 1)
        from_below = shifted(light[:, :margin], "tile", -1)
        middle = light[:, margin : margin + strip]
        middle = jnp.concatenate(
            [middle[:, :margin] + from_above, middle[:, margin:-margin], middle[:, -margin:] + from_below], axis=1
        )
        pieces.append(scatter_sum(middle, "wave", g % 2 == 0))
    colour = jnp.concatenate(pieces, axis=2)
    return colour[:, :, margin : margin + tile_cols * side]


def solution(mesh):
    in_specs = (
        P("wave", "tile", None),
        P("wave", "tile", None, None, None),
        P("tile", None, None),
        P("tile", None, None),
        P(),
    )
    out_specs = P(None, ("tile", "wave"), None)
    return jax.shard_map(
        per_device, mesh=mesh, in_specs=in_specs, out_specs=out_specs, check_vma=False
    )
```

time: 688 us -> 178 us (0.26)
  matrix products: 350 us -> 0 us
  waiting for transfers between devices: 202 us -> 65.2 us
  Pallas kernels: 0 us -> 66.9 us
  local copies, waits for them, and re-layouts: 74.2 us -> 14.4 us
  loops' own time: 16.7 us -> 0 us
  between operations: 14.5 us -> 0.26 us
  starting transfers between devices: 9.38 us -> 22 us
  other arithmetic: 17.4 us -> 8.53 us
    dot_general x149 -> x0, matrix products: 350 us -> none  [the longest x16 41.1 us: forward(): jnp.einsum('tkb,bl->tkl', row_imag, sin_top, precision=highest)]
    unnamed x2 -> x0, waiting for transfers between devices: 156 us -> none
    pallas_call x0 -> x3, Pallas kernels: none -> 66.9 us  [the longest x2 54.6 us: colour_columns(): pl.pallas_call(functools.partial(colour_kernel, dims), grid=(steps,), in_...]
    dynamic_slice x36 -> x5, local copies, waits for them, and re-layouts: 23.6 us -> 0.88 us  [the longest x1 0.65 us: per_device(): lax.dynamic_slice_in_dim(response, lax.axis_index('wave') * waves, waves, 1)]
    ppermute x4 -> x12, waiting for transfers between devices: 45.2 us -> 65.2 us  [the longest x6 51.9 us: scatter_sum(): lax.ppermute(give, axis, [(i, i ^ 1 << bit) for i in range(size)])]
    another operation x5 -> x0, loops' own time: 16.7 us -> none  [the longest x4 10.2 us: blur_wave(): rows_out = lax.map(one_row, (scene_rows, psf_set))]
    slice x15 -> x4, local copies, waits for them, and re-layouts: 18.2 us -> 4.3 us  [the longest x2 3.04 us: per_device(): from_above = shifted(light[:, strip + margin:], 'tile', 1)]
    dynamic_update_slice x12 -> x0, local copies, waits for them, and re-layouts: 13.7 us -> none  [the longest x8 8.5 us: blur_wave(): rows_out = lax.map(one_row, (scene_rows, psf_set))]
  transfers between devices with their start and end apart: 5 -> 12, of which waited for: 5 -> 11; matrix products, arithmetic and copies ran while one was open for 1% -> 9% of each run, Pallas kernels for 0% -> 23%
where the time goes in v1:
time: 178 us; the launch traced here: 177 us
  Pallas kernels  66.9 us (38%)
  waiting for transfers between devices  65.2 us (37%)
  starting transfers between devices  22 us (12%)
  local copies, waits for them, and re-layouts  14.4 us (8%)
  other arithmetic  8.53 us (5%)
    pallas_call x2, Pallas kernels, colour_columns(): pl.pallas_call(functools.partial(colour_kernel, dims), grid=(steps,), in_...  54.6 us
    ppermute x6, waiting for transfers between devices, scatter_sum(): lax.ppermute(give, axis, [(i, i ^ 1 << bit) for i in range(size)])  51.9 us
    ppermute x6, starting transfers between devices, shifted(): lax.ppermute(values, axis, [(i, i + by) for i in range(size) if 0 <= i +...  15.1 us
    ppermute x6, waiting for transfers between devices, shifted(): lax.ppermute(values, axis, [(i, i + by) for i in range(size) if 0 <= i +...  13.3 us
    pallas_call x1, Pallas kernels, scene_spectra(): pl.pallas_call(functools.partial(scene_kernel, side, tile_cols), grid=(wa...  12.3 us
    ppermute x6, starting transfers between devices, scatter_sum(): lax.ppermute(give, axis, [(i, i ^ 1 << bit) for i in range(size)])  6.9 us
    squeeze x1, local copies, waits for them, and re-layouts, per_device(): below = shifted(bank[:, 0], 'tile', -1)  4.7 us
  transfers between devices with their start and end apart: 12, of which 11 were waited for; matrix products, arithmetic and copies ran while one was open for 9% of the time, Pallas kernels for 23%

profile of v1, /device:TPU:4, one launch (start us, length us, event | category | flops | bytes accessed | tf_op | source)
XLA Modules:
  0.0 177.3 jit_solution(8737116274646451004)
XLA Ops:
  0.0 4.7 %slice_bitcast_fusion = (f32[4,8,128,128]{3,2,1,0:T(8,128)}, f32[4,8,128,128]{3,2,1,0:T(8,128)}) fusion(f32[4,2,8,128,128]{4,3,2,1,0:T(8,128)} %param.16), kind=kLoop, calls=%fused_computation | loop fusion | bytes 8388608 | tf_op jit(solution)/shard_map/squeeze | solution.py:330
  4.7 1.9 %collective-permute-start = (f32[4,8,128,128]{3,2,1,0:T(8,128)}, f32[4,8,128,128]{3,2,1,0:T(8,128)S(1)}, u32[]{:S(2)}, u32[]{:S(2)}) collective-permute-start(f32[4,8,128,128]{3,2,1,0:T(8,128)} %get-tuple-element.12), channel_id=1, source_target_pairs={{0,1},{1,2},{2,3},{4,5},{5,6},{6,7},{8,9},{9,10},{10,11},{12,13},{... | collective-permute-start | bytes 6291464 | tf_op jit(solution)/shard_map/ppermute | solution.py:302
  6.6 3.6 %collective-permute-start.1 = (f32[4,8,128,128]{3,2,1,0:T(8,128)}, f32[4,8,128,128]{3,2,1,0:T(8,128)}, u32[]{:S(2)}, u32[]{:S(2)}) collective-permute-start(f32[4,8,128,128]{3,2,1,0:T(8,128)} %get-tuple-element.11), channel_id=1, source_target_pairs={{1,0},{2,1},{3,2},{5,4},{6,5},{7,6},{9,8},{10,9},{11,10},{13,12},{... | collective-permute-start | bytes 6291464 | tf_op jit(solution)/shard_map/ppermute | solution.py:302
  12.4 12.3 %scene_spectra.1.spec_ref = f32[4,2,8,256,256]{4,3,2,1,0:T(8,128)} custom-call(bf16[256,384]{1,0:T(8,128)(2,1)} %constant.76.clone.rows_ref.rows_in, bf16[384,256]{1,0:T(8,128)(2,1)} %constant.77.clone.cols_ref.cols_in, f32[4,256,1024]{2,1,0:T(8,128)} %scene_ref.1), custom_call_target="tpu_custom_call" | custom-call | flops 3221225472 | bytes 20971520 | tf_op jit(solution)/shard_map/scene_spectra/pallas_call | solution.py:91
  24.8 7.5 %collective-permute-done.above_ref = f32[4,8,128,128]{3,2,1,0:T(8,128)S(1)} collective-permute-done((f32[4,8,128,128]{3,2,1,0:T(8,128)}, f32[4,8,128,128]{3,2,1,0:T(8,128)S(1)}, u32[]{:S(2)}, u32[]{:S(2)}) %collective-permute-start) | collective-permute-done | bytes 2097184 | tf_op jit(solution)/shard_map/ppermute | solution.py:302
  32.3 1.9 %collective-permute-done.1.below_ref = f32[4,8,128,128]{3,2,1,0:T(8,128)} collective-permute-done((f32[4,8,128,128]{3,2,1,0:T(8,128)}, f32[4,8,128,128]{3,2,1,0:T(8,128)}, u32[]{:S(2)}, u32[]{:S(2)}) %collective-permute-start.1) | collective-permute-done | bytes 2097184 | tf_op jit(solution)/shard_map/ppermute | solution.py:302
  35.1 26.9 %colour_columns.2 = (f32[3,384,512]{2,1,0:T(8,128)}, f32[2,768,128]{2,1,0:T(8,128)}) custom-call(s32[64]{0:T(128)} %reshape.15.slot_ref, f32[64]{0:T(128)} %reshape.16.weight_ref, f32[3,4]{1,0:T(4,128)} %constant_dynamic-slice_fusion.4.response_ref, bf16[256,384]{1,0:T(8,128)(2,1)} %constant.76.clone.rows_ref.rows_in, ...), custom_call_target="tpu_custom_call" | custom-call | flops 5234491392 | bytes 8388608 | tf_op jit(solution)/shard_map/colour_columns/pallas_call | solution.py:252
  63.1 1.9 %collective-permute-start.2 = (f32[3,64,512]{2,1,0:T(8,128)S(1)}, f32[3,64,512]{2,1,0:T(8,128)S(1)}, u32[]{:S(2)}, u32[]{:S(2)}) collective-permute-start(f32[3,64,512]{2,1,0:T(8,128)S(1)} %slice.50), channel_id=1, source_target_pairs={{0,1},{1,2},{2,3},{4,5},{5,6},{6,7},{8,9},{9,10},{10,11},{12,13},{... | collective-permute-start | bytes 1179656 | tf_op jit(solution)/shard_map/ppermute | solution.py:302
  65.0 27.6 %colour_columns.3 = (f32[3,384,640]{2,1,0:T(8,128)}, f32[2,768,128]{2,1,0:T(8,128)}) custom-call(s32[64]{0:T(128)} %reshape.15.slot_ref, f32[64]{0:T(128)} %reshape.16.weight_ref, f32[3,4]{1,0:T(4,128)} %constant_dynamic-slice_fusion.4.response_ref, bf16[256,384]{1,0:T(8,128)(2,1)} %constant.76.clone.rows_ref.rows_in, ...), custom_call_target="tpu_custom_call" | custom-call | flops 5234491392 | bytes 8388608 | tf_op jit(solution)/shard_map/colour_columns/pallas_call | solution.py:252
  92.6 2.0 %slice.55 = f32[3,64,640]{2,1,0:T(8,128)} slice(f32[3,384,640]{2,1,0:T(8,128)} %get-tuple-element.10), slice={[0:3], [320:384], [0:640]} | slice | bytes 983040 | tf_op jit(solution)/shard_map/slice | solution.py:345
  94.6 1.9 %collective-permute-start.7 = (f32[3,64,640]{2,1,0:T(8,128)}, f32[3,64,640]{2,1,0:T(8,128)S(1)}, u32[]{:S(2)}, u32[]{:S(2)}) collective-permute-start(f32[3,64,640]{2,1,0:T(8,128)} %slice.55), channel_id=1, source_target_pairs={{0,1},{1,2},{2,3},{4,5},{5,6},{6,7},{8,9},{9,10},{10,11},{12,13},{... | collective-permute-start | bytes 1474568 | tf_op jit(solution)/shard_map/ppermute | solution.py:302
  96.6 2.1 %slice_add_fusion.3 = (f32[3,64,512]{2,1,0:T(8,128)}, f32[3,64,512]{2,1,0:T(8,128)}) fusion(f32[3,64,512]{2,1,0:T(8,128)S(1)} %collective-permute-done.2, f32[3,384,512]{2,1,0:T(8,128)} %get-tuple-element.8), kind=kLoop, calls=%fused_computation.16 | loop fusion | flops 98304 | bytes 1966080 | tf_op jit(solution)/shard_map/add | solution.py:349
  98.7 3.8 %collective-permute-start.3 = (f32[3,64,512]{2,1,0:T(8,128)}, f32[3,64,512]{2,1,0:T(8,128)}, u32[]{:S(2)}, u32[]{:S(2)}) collective-permute-start(f32[3,64,512]{2,1,0:T(8,128)} %get-tuple-element.16), channel_id=1, source_target_pairs={{1,0},{2,1},{3,2},{5,4},{6,5},{7,6},{9,8},{10,9},{11,10},{13,12},{... | collective-permute-start | bytes 1179656 | tf_op jit(solution)/shard_map/ppermute | solution.py:302
  102.5 1.2 slice.51
  103.8 1.4 collective-permute-done.7
  105.3 1.9 %collective-permute-start.8 = (f32[3,64,640]{2,1,0:T(8,128)S(1)}, f32[3,64,640]{2,1,0:T(8,128)S(1)}, u32[]{:S(2)}, u32[]{:S(2)}) collective-permute-start(f32[3,64,640]{2,1,0:T(8,128)S(1)} %get-tuple-element.14), channel_id=1, source_target_pairs={{1,0},{2,1},{3,2},{5,4},{6,5},{7,6},{9,8},{10,9},{11,10},{13,12},{... | collective-permute-start | bytes 1474568 | tf_op jit(solution)/shard_map/ppermute | solution.py:302
  108.1 1.2 slice_add_fusion.2
  110.4 1.5 collective-permute-start.4
  111.9 1.6 collective-permute-done.8
  113.5 1.1 slice_add_fusion
  114.7 1.1 dynamic-slice_bitcast_fusion
  115.8 1.6 collective-permute-start.9
  117.4 12.4 %collective-permute-done.4 = f32[3,2,2,32,512]{4,3,2,1,0:T(8,128)} collective-permute-done((f32[3,2,2,32,512]{4,3,2,1,0:T(8,128)}, f32[3,2,2,32,512]{4,3,2,1,0:T(8,128)}, u32[]{:S(2)}, u32[]{:S(2)}) %collective-permute-start.4) | collective-permute-done | bytes 786464 | tf_op jit(solution)/shard_map/ppermute | solution.py:318
  129.8 1.3 bitcast_add_fusion.1
  131.2 1.6 collective-permute-start.5
  132.9 13.2 %collective-permute-done.9 = f32[3,2,2,32,640]{4,3,2,1,0:T(8,128)} collective-permute-done((f32[3,2,2,32,640]{4,3,2,1,0:T(8,128)}, f32[3,2,2,32,640]{4,3,2,1,0:T(8,128)}, u32[]{:S(2)}, u32[]{:S(2)}) %collective-permute-start.9) | collective-permute-done | bytes 983072 | tf_op jit(solution)/shard_map/ppermute | solution.py:318
  146.1 1.4 bitcast_add_fusion
  147.7 3.4 %collective-permute-done.5 = f32[3,2,32,512]{3,2,0,1:T(8,128)S(1)} collective-permute-done((f32[3,2,32,512]{3,2,0,1:T(8,128)S(1)}, f32[3,2,32,512]{3,2,0,1:T(8,128)S(1)}, u32[]{:S(2)}, u32[]{:S(2)}) %collective-permute-start.5) | collective-permute-done | bytes 393248 | tf_op jit(solution)/shard_map/ppermute | solution.py:318
  151.2 1.8 collective-permute-start.6
  152.9 17.0 %collective-permute-done.10 = f32[3,2,32,640]{3,2,0,1:T(8,128)S(1)} collective-permute-done((f32[3,2,32,640]{3,2,0,1:T(8,128)S(1)}, f32[3,2,32,640]{3,2,0,1:T(8,128)S(1)}, u32[]{:S(2)}, u32[]{:S(2)}) %collective-permute-start.10) | collective-permute-done | bytes 491552 | tf_op jit(solution)/shard_map/ppermute | solution.py:318
  170.4 1.7 collective-permute-done.6
  172.1 4.2 %collective-permute-done.11 = f32[3,32,640]{2,1,0:T(8,128)S(1)} collective-permute-done((f32[3,32,640]{2,1,0:T(8,128)S(1)}, f32[3,32,640]{2,1,0:T(8,128)S(1)}, u32[]{:S(2)}, u32[]{:S(2)}) %collective-permute-start.11) | collective-permute-done | bytes 245792 | tf_op jit(solution)/shard_map/ppermute | solution.py:318
  (41 shorter events, 8.3 us)
Async XLA Ops:
  0.0 11.8 %copy-start = (f32[3,32]{1,0:T(4,128)S(1)}, f32[3,32]{1,0:T(4,128)}, u32[]{:S(2)}) copy-start(f32[3,32]{1,0:T(4,128)} %param.19) | copy-start | bytes 1156
  0.0 10.3 %copy-start.4 = (s32[2,8,4]{1,2,0:T(4,128)S(1)}, s32[2,8,4]{1,2,0:T(4,128)}, u32[]{:S(2)}) copy-start(s32[2,8,4]{1,2,0:T(4,128)} %param.17) | copy-start | bytes 772
  0.0 11.1 %copy-start.5 = (s32[2,8,4]{1,2,0:T(4,128)S(1)}, s32[2,8,4]{1,2,0:T(4,128)}, u32[]{:S(2)}) copy-start(s32[2,8,4]{1,2,0:T(4,128)} %param.18) | copy-start | bytes 772
  4.7 27.6 %collective-permute-start = (f32[4,8,128,128]{3,2,1,0:T(8,128)}, f32[4,8,128,128]{3,2,1,0:T(8,128)S(1)}, u32[]{:S(2)}, u32[]{:S(2)}) collective-permute-start(f32[4,8,128,128]{3,2,1,0:T(8,128)} %get-tuple-element.12), channel_id=1, source_target_pairs={{0,1},{1,2},{2,3},{4,5},{5,6},{6,7},{8,9},{9,10},{10,11},{12,13},{... | collective-permute-start | bytes 6291464 | tf_op jit(solution)/shard_map/ppermute | solution.py:302
  6.6 27.5 %collective-permute-start.1 = (f32[4,8,128,128]{3,2,1,0:T(8,128)}, f32[4,8,128,128]{3,2,1,0:T(8,128)}, u32[]{:S(2)}, u32[]{:S(2)}) collective-permute-start(f32[4,8,128,128]{3,2,1,0:T(8,128)} %get-tuple-element.11), channel_id=1, source_target_pairs={{1,0},{2,1},{3,2},{5,4},{6,5},{7,6},{9,8},{10,9},{11,10},{13,12},{... | collective-permute-start | bytes 6291464 | tf_op jit(solution)/shard_map/ppermute | solution.py:302
  32.3 2.8 %copy-start.1 = (f32[4,8,128,128]{3,2,1,0:T(8,128)}, f32[4,8,128,128]{3,2,1,0:T(8,128)S(1)}, u32[]{:S(2)}) copy-start(f32[4,8,128,128]{3,2,1,0:T(8,128)S(1)} %collective-permute-done.above_ref) | copy-start | bytes 6291460
  63.1 33.5 %collective-permute-start.2 = (f32[3,64,512]{2,1,0:T(8,128)S(1)}, f32[3,64,512]{2,1,0:T(8,128)S(1)}, u32[]{:S(2)}, u32[]{:S(2)}) collective-permute-start(f32[3,64,512]{2,1,0:T(8,128)S(1)} %slice.50), channel_id=1, source_target_pairs={{0,1},{1,2},{2,3},{4,5},{5,6},{6,7},{8,9},{9,10},{10,11},{12,13},{... | collective-permute-start | bytes 1179656 | tf_op jit(solution)/shard_map/ppermute | solution.py:302
  92.6 11.1 %copy-start.2 = (f32[3,384,640]{2,1,0:T(8,128)S(1)}, f32[3,384,640]{2,1,0:T(8,128)}, u32[]{:S(2)}) copy-start(f32[3,384,640]{2,1,0:T(8,128)} %get-tuple-element.10) | copy-start | bytes 8847364
  94.6 10.5 %collective-permute-start.7 = (f32[3,64,640]{2,1,0:T(8,128)}, f32[3,64,640]{2,1,0:T(8,128)S(1)}, u32[]{:S(2)}, u32[]{:S(2)}) collective-permute-start(f32[3,64,640]{2,1,0:T(8,128)} %slice.55), channel_id=1, source_target_pairs={{0,1},{1,2},{2,3},{4,5},{5,6},{6,7},{8,9},{9,10},{10,11},{12,13},{... | collective-permute-start | bytes 1474568 | tf_op jit(solution)/shard_map/ppermute | solution.py:302
  98.7 9.4 %collective-permute-start.3 = (f32[3,64,512]{2,1,0:T(8,128)}, f32[3,64,512]{2,1,0:T(8,128)}, u32[]{:S(2)}, u32[]{:S(2)}) collective-permute-start(f32[3,64,512]{2,1,0:T(8,128)} %get-tuple-element.16), channel_id=1, source_target_pairs={{1,0},{2,1},{3,2},{5,4},{6,5},{7,6},{9,8},{10,9},{11,10},{13,12},{... | collective-permute-start | bytes 1179656 | tf_op jit(solution)/shard_map/ppermute | solution.py:302
  103.8 5.5 %copy-start.3 = (f32[3,64,512]{2,1,0:T(8,128)S(1)}, f32[3,64,512]{2,1,0:T(8,128)}, u32[]{:S(2)}) copy-start(f32[3,64,512]{2,1,0:T(8,128)} %get-tuple-element.15) | copy-start | bytes 1179652
  105.3 8.3 %collective-permute-start.8 = (f32[3,64,640]{2,1,0:T(8,128)S(1)}, f32[3,64,640]{2,1,0:T(8,128)S(1)}, u32[]{:S(2)}, u32[]{:S(2)}) collective-permute-start(f32[3,64,640]{2,1,0:T(8,128)S(1)} %get-tuple-element.14), channel_id=1, source_target_pairs={{1,0},{2,1},{3,2},{5,4},{6,5},{7,6},{9,8},{10,9},{11,10},{13,12},{... | collective-permute-start | bytes 1474568 | tf_op jit(solution)/shard_map/ppermute | solution.py:302
  110.4 19.4 %collective-permute-start.4 = (f32[3,2,2,32,512]{4,3,2,1,0:T(8,128)}, f32[3,2,2,32,512]{4,3,2,1,0:T(8,128)}, u32[]{:S(2)}, u32[]{:S(2)}) collective-permute-start(f32[3,2,2,32,512]{4,3,2,1,0:T(8,128)} %dynamic-slice_bitcast_fusion.1), channel_id=1, source_target_pairs={{0,4},{4,0},{8,12},{12,8},{16,20},{20,16},{24,28},{28,24},{1,5},{5... | collective-permute-start | bytes 2359304 | tf_op jit(solution)/shard_map/ppermute | solution.py:318
  115.8 30.3 %collective-permute-start.9 = (f32[3,2,2,32,640]{4,3,2,1,0:T(8,128)}, f32[3,2,2,32,640]{4,3,2,1,0:T(8,128)}, u32[]{:S(2)}, u32[]{:S(2)}) collective-permute-start(f32[3,2,2,32,640]{4,3,2,1,0:T(8,128)} %dynamic-slice_bitcast_fusion), channel_id=1, source_target_pairs={{0,8},{4,12},{8,0},{12,4},{16,24},{20,28},{24,16},{28,20},{1,9},{5... | collective-permute-start | bytes 2949128 | tf_op jit(solution)/shard_map/ppermute | solution.py:318
  131.2 19.8 %collective-permute-start.5 = (f32[3,2,32,512]{3,2,0,1:T(8,128)S(1)}, f32[3,2,32,512]{3,2,0,1:T(8,128)S(1)}, u32[]{:S(2)}, u32[]{:S(2)}) collective-permute-start(f32[3,2,32,512]{3,2,0,1:T(8,128)S(1)} %bitcast.46), channel_id=1, source_target_pairs={{0,8},{4,12},{8,0},{12,4},{16,24},{20,28},{24,16},{28,20},{1,9},{5... | collective-permute-start | bytes 1179656 | tf_op jit(solution)/shard_map/ppermute | solution.py:318
  147.6 22.4 %collective-permute-start.10 = (f32[3,2,32,640]{3,2,0,1:T(8,128)S(1)}, f32[3,2,32,640]{3,2,0,1:T(8,128)S(1)}, u32[]{:S(2)}, u32[]{:S(2)}) collective-permute-start(f32[3,2,32,640]{3,2,0,1:T(8,128)S(1)} %bitcast.45), channel_id=1, source_target_pairs={{0,16},{4,20},{8,24},{12,28},{16,0},{20,4},{24,8},{28,12},{1,17},{... | collective-permute-start | bytes 1474568 | tf_op jit(solution)/shard_map/ppermute | solution.py:318
  151.2 20.9 %collective-permute-start.6 = (f32[3,32,512]{2,1,0:T(8,128)S(1)}, f32[3,32,512]{2,1,0:T(8,128)S(1)}, u32[]{:S(2)}, u32[]{:S(2)}) collective-permute-start(f32[3,32,512]{2,1,0:T(8,128)S(1)} %dynamic-slice_bitcast_fusion.3), channel_id=1, source_target_pairs={{0,16},{4,20},{8,24},{12,28},{16,0},{20,4},{24,8},{28,12},{1,17},{... | collective-permute-start | bytes 589832 | tf_op jit(solution)/shard_map/ppermute | solution.py:318
  170.1 6.3 %collective-permute-start.11 = (f32[3,32,640]{2,1,0:T(8,128)S(1)}, f32[3,32,640]{2,1,0:T(8,128)S(1)}, u32[]{:S(2)}, u32[]{:S(2)}) collective-permute-start(f32[3,32,640]{2,1,0:T(8,128)S(1)} %dynamic-slice_bitcast_fusion.2), channel_id=1, source_target_pairs={{0,4},{4,0},{8,12},{12,8},{16,20},{20,16},{24,28},{28,24},{1,5},{5... | collective-permute-start | bytes 737288 | tf_op jit(solution)/shard_map/ppermute | solution.py:318

commit v2 on v0

v2 whole, which is shorter than its diff:
```python
import functools

import jax
import jax.numpy as jnp
import ml_dtypes
import numpy as np
from jax import lax
from jax.experimental import pallas as pl
from jax.experimental.pallas import tpu as pltpu
from jax.sharding import PartitionSpec as P

CHUNK_ROWS = 16
VMEM_BYTES = 56 * 1024 * 1024


def halves(table):
    high = table.astype(ml_dtypes.bfloat16)
    low = (table - high.astype(np.float64)).astype(ml_dtypes.bfloat16)
    return high, low


def left_factor(table):
    high, low = halves(table)
    return np.concatenate([high, high, low], axis=1)


def right_factor(table):
    high, low = halves(table)
    return np.concatenate([high, high, low], axis=0)


def tables(side):
    length = 2 * side
    odd = 2 * np.arange(side)[:, None] + 1
    angle = np.pi * (odd * np.arange(length)[None, :] % (2 * length)) / length
    cosine, sine = np.cos(angle), np.sin(angle)
    rows_in = np.concatenate([cosine[:, :side], -sine[:, :side]], axis=0)
    cols_in = np.concatenate([cosine[:, :side].T, sine[:, :side].T], axis=1)
    cols_out = np.concatenate([cosine, sine], axis=0)
    rows_out = np.concatenate([cosine.T, -sine.T], axis=1) * (2.0 / (length * length))
    return left_factor(rows_in), right_factor(cols_in), right_factor(cols_out), left_factor(rows_out)


def split(values):
    high = values.astype(jnp.bfloat16)
    low = (values - high.astype(jnp.float32)).astype(jnp.bfloat16)
    return high, low


def dot(left, right):
    return jnp.dot(left, right, preferred_element_type=jnp.float32)


def put_rows(out_ref, values, side, lanes):
    high, low = split(values)
    out_ref[0:side, lanes] = high
    out_ref[side : 2 * side, lanes] = low
    out_ref[2 * side : 3 * side, lanes] = high


def put_cols(out_ref, values, width, rows):
    high, low = split(values)
    out_ref[rows, 0:width] = high
    out_ref[rows, width : 2 * width] = low
    out_ref[rows, 2 * width : 3 * width] = high


def camera_kernel(
    dims,
    weight_ref,
    response_ref,
    rows_in,
    cols_in,
    cols_out,
    rows_out,
    scene_ref,
    bank_ref,
    out_ref,
    above,
    below,
    carry,
    lifted,
    lift_mid,
    scene_spec,
    psf_spec,
    mixed,
    back,
    light,
    light_above,
    light_below,
    middle,
    got_low,
    part,
    got_high,
    bank_sent,
    bank_got,
    light_sent,
    light_got,
    low_sent,
    low_got,
    high_sent,
    high_got,
):
    tile_count, low_count, high_count, tile_rows, tile_cols, side, waves, channels = dims
    step = pl.program_id(0)
    length, margin, strip = 2 * side, side // 2, tile_rows * side
    slab = strip // (low_count * high_count)
    blocks = tile_cols + 1
    tile, wave = lax.axis_index("tile"), lax.axis_index("wave")
    low, high = lax.rem(wave, low_count), lax.div(wave, low_count)
    has_above, has_below = tile > 0, tile < tile_count - 1
    tile_above = lax.rem(tile + tile_count - 1, tile_count)
    tile_below = lax.rem(tile + 1, tile_count)

    def remote(src, dst, sent, got, axis, index):
        return pltpu.make_async_remote_copy(
            src_ref=src,
            dst_ref=dst,
            send_sem=sent,
            recv_sem=got,
            device_id={axis: index},
            device_id_type=pl.DeviceIdType.MESH,
        )

    def bank_down(c):
        return remote(
            bank_ref.at[:, tile_rows - 1, c], above.at[c], bank_sent.at[0, c], bank_got.at[0, c], "tile", tile_below
        )

    def bank_up(c):
        return remote(bank_ref.at[:, 0, c], below.at[c], bank_sent.at[1, c], bank_got.at[1, c], "tile", tile_above)

    def light_down(b):
        return remote(
            light.at[b, :, pl.ds(strip + margin, margin)],
            light_above.at[b],
            light_sent.at[0, b],
            light_got.at[0, b],
            "tile",
            tile_below,
        )

    def light_up(b):
        return remote(
            light.at[b, :, pl.ds(0, margin)], light_below.at[b], light_sent.at[1, b], light_got.at[1, b], "tile", tile_above
        )

    def start_pair(down, up):
        @pl.when(has_below)
        def _():
            down.start()

        @pl.when(has_above)
        def _():
            up.start()

    def wait_pair(down, up):
        @pl.when(has_below)
        def _():
            down.wait_send()
            up.wait_recv()

        @pl.when(has_above)
        def _():
            up.wait_send()
            down.wait_recv()

    def low_peer(d):
        return lax.rem(low + d, low_count)

    def high_peer(d):
        return lax.rem(high + d, high_count)

    def to_low(b, d):
        peer = low_peer(d)
        return remote(
            middle.at[b, peer],
            got_low.at[b, d - 1],
            low_sent.at[b, d - 1],
            low_got.at[b, d - 1],
            "wave",
            high * low_count + peer,
        )

    def to_high(b, d):
        peer = high_peer(d)
        return remote(
            part.at[b, peer],
            got_high.at[b, d - 1],
            high_sent.at[b, d - 1],
            high_got.at[b, d - 1],
            "wave",
            peer * low_count + low,
        )

    @pl.when(step == 0)
    def _():
        barrier = pltpu.get_barrier_semaphore()

        def greet(axis, index):
            pl.semaphore_signal(barrier, inc=1, device_id={axis: index}, device_id_type=pl.DeviceIdType.MESH)

        for d in range(1, low_count):
            greet("wave", high * low_count + low_peer(d))
        for d in range(1, high_count):
            greet("wave", high_peer(d) * low_count + low)

        @pl.when(has_above)
        def _():
            greet("tile", tile_above)

        @pl.when(has_below)
        def _():
            greet("tile", tile_below)

        others = low_count + high_count - 2
        pl.semaphore_wait(barrier, others + has_above.astype(jnp.int32) + has_below.astype(jnp.int32))
        for c in range(min(3, tile_cols)):
            start_pair(bank_down(c), bank_up(c))
        carry[...] = jnp.zeros_like(carry)

        @pl.when(jnp.logical_not(has_above))
        def _():
            above[...] = jnp.zeros_like(above)
            light_above[...] = jnp.zeros_like(light_above)

        @pl.when(jnp.logical_not(has_below))
        def _():
            below[...] = jnp.zeros_like(below)
            light_below[...] = jnp.zeros_like(light_below)

    @pl.when(jnp.logical_and(step > 0, step + 2 < tile_cols))
    def _():
        start_pair(bank_down(step + 2), bank_up(step + 2))

    def transform(spec):
        first = dot(rows_in[...], lifted[...])
        for t in range(tile_rows * waves):
            put_cols(lift_mid, first[:, t * side : (t + 1) * side], side, slice(t * length, (t + 1) * length))
        spec[...] = dot(lift_mid[...], cols_in[...])

    @pl.when(step < tile_cols)
    def _():
        for r in range(tile_rows):
            for w in range(waves):
                lane = (r * waves + w) * side
                put_rows(lifted, scene_ref[w, r * side : (r + 1) * side, :], side, slice(lane, lane + side))
        transform(scene_spec)

        @pl.when(step == 0)
        def _():
            wait_pair(bank_down(0), bank_up(0))

        @pl.when(step + 1 < tile_cols)
        def _():
            wait_pair(bank_down(step + 1), bank_up(step + 1))

        near = (jnp.maximum(step - 1, 0), step, jnp.minimum(step + 1, tile_cols - 1))
        for r in range(tile_rows):
            place = (r * tile_cols + step) * 9
            for w in range(waves):
                psf = None
                for i in range(3):
                    for j in range(3):
                        row = r + i - 1
                        if row < 0:
                            field = above[near[j], w]
                        elif row >= tile_rows:
                            field = below[near[j], w]
                        else:
                            field = bank_ref[w, row, near[j]]
                        term = weight_ref[place + 3 * i + j] * field
                        psf = term if psf is None else psf + term
                lane = (r * waves + w) * side
                put_rows(lifted, psf, side, slice(lane, lane + side))
        transform(psf_spec)

        def some_rows(r, index, state):
            start = pl.multiple_of(index * CHUNK_ROWS, CHUNK_ROWS)
            left, right = slice(0, side), slice(side, length)
            sums = [None] * channels
            for w in range(waves):
                upper = pl.ds(start + (r * waves + w) * length, CHUNK_ROWS)
                lower = pl.ds(start + (r * waves + w) * length + side, CHUNK_ROWS)
                a, b, d, e = psf_spec[upper, left], psf_spec[upper, right], psf_spec[lower, left], psf_spec[lower, right]
                p1r, p1i, p2r, p2i = a + e, d - b, a - e, d + b
                a, b, d, e = (
                    scene_spec[upper, left],
                    scene_spec[upper, right],
                    scene_spec[lower, left],
                    scene_spec[lower, right],
                )
                s1r, s1i, s2r, s2i = a + e, d - b, a - e, d + b
                q1r, q1i = s1r * p1r - s1i * p1i, s1r * p1i + s1i * p1r
                q2r, q2i = s2r * p2r - s2i * p2i, s2r * p2i + s2i * p2r
                parts = (q1r + q2r, q2i - q1i, q1i + q2i, q1r - q2r)
                for ch in range(channels):
                    gain = response_ref[ch, w]
                    terms = [gain * value for value in parts]
                    sums[ch] = terms if w == 0 else [old + new for old, new in zip(sums[ch], terms)]
            for ch in range(channels):
                top = start + (r * channels + ch) * length
                for j, rows in ((0, pl.ds(top, CHUNK_ROWS)), (2, pl.ds(top + side, CHUNK_ROWS))):
                    for h in range(2):
                        upper_bits, lower_bits = split(sums[ch][j + h])
                        mixed[rows, h * side : (h + 1) * side] = upper_bits
                        mixed[rows, length + h * side : length + (h + 1) * side] = lower_bits
                        mixed[rows, 2 * length + h * side : 2 * length + (h + 1) * side] = upper_bits
            return state

        for r in range(tile_rows):
            lax.fori_loop(0, side // CHUNK_ROWS, functools.partial(some_rows, r), 0)
        partial = dot(mixed[...], cols_out[...])
        for r in range(tile_rows):
            for ch in range(channels):
                rows = slice((r * channels + ch) * length, (r * channels + ch + 1) * length)
                lane = (r * channels + ch) * side
                put_rows(back, partial[rows, 0:side] + carry[rows, :], length, slice(lane, lane + side))
                carry[rows, :] = partial[rows, side:length]

    @pl.when(step == tile_cols)
    def _():
        for r in range(tile_rows):
            for ch in range(channels):
                rows = slice((r * channels + ch) * length, (r * channels + ch + 1) * length)
                lane = (r * channels + ch) * side
                put_rows(back, carry[rows, :], length, slice(lane, lane + side))

    @pl.when(step < blocks)
    def _():
        rays = dot(rows_out[...], back[...])
        for ch in range(channels):
            for r in range(tile_rows + 1):
                total = None
                if r < tile_rows:
                    lane = (r * channels + ch) * side
                    total = rays[0:side, lane : lane + side]
                if r > 0:
                    lane = ((r - 1) * channels + ch) * side
                    tail = rays[side:length, lane : lane + side]
                    total = tail if total is None else total + tail
                light[step, ch, r * side : (r + 1) * side, :] = total
        start_pair(light_down(step), light_up(step))

    @pl.when(jnp.logical_and(step >= 1, step < blocks + 1))
    def _():
        b = step - 1
        wait_pair(light_down(b), light_up(b))
        for ch in range(channels):
            for h in range(high_count):
                for o in range(low_count):
                    start = (h * low_count + o) * slab
                    value = light[b, ch, margin + start : margin + start + slab, :]
                    if start < margin:
                        value = value + light_above[b, ch, start : start + slab, :]
                    if start >= strip - margin:
                        start = start - (strip - margin)
                        value = value + light_below[b, ch, start : start + slab, :]
                    middle[b, o, h, ch] = value
        for d in range(1, low_count):
            to_low(b, d).start()

    @pl.when(jnp.logical_and(step >= 2, step < blocks + 2))
    def _():
        b = step - 2
        for d in range(1, low_count):
            to_low(b, d).wait()
        total = middle[b, low]
        for d in range(1, low_count):
            total = total + got_low[b, d - 1]
        part[b] = total
        for d in range(1, high_count):
            to_high(b, d).start()

    @pl.when(step >= 3)
    def _():
        b = step - 3
        for d in range(1, high_count):
            to_high(b, d).wait()
        total = part[b, high]
        for d in range(1, high_count):
            total = total + got_high[b, d - 1]
        out_ref[b] = total


def camera(scene, bank, weights, response, tile_count, wave_count):
    waves, tile_rows, tile_cols, side = bank.shape[:4]
    channels = response.shape[0]
    length, strip, margin = 2 * side, tile_rows * side, side // 2
    blocks = tile_cols + 1
    low_count = 1 << ((wave_count.bit_length() - 1) // 2)
    high_count = wave_count // low_count
    slab = strip // wave_count
    factors = tables(side)
    dims = (tile_count, low_count, high_count, tile_rows, tile_cols, side, waves, channels)
    smem = pl.BlockSpec(memory_space=pltpu.SMEM)
    vmem = pl.BlockSpec(memory_space=pltpu.VMEM)
    f32, bf16, sems = jnp.float32, jnp.bfloat16, pltpu.SemaphoreType.DMA
    tiles = tile_rows * waves
    planes = tile_rows * channels
    return pl.pallas_call(
        functools.partial(camera_kernel, dims),
        grid=(blocks + 3,),
        in_specs=[
            smem,
            smem,
            vmem,
            vmem,
            vmem,
            vmem,
            pl.BlockSpec((waves, strip, side), lambda s: (0, 0, jnp.minimum(s, tile_cols - 1))),
            vmem,
        ],
        out_specs=vmem,
        out_shape=jax.ShapeDtypeStruct((blocks, channels, slab, side), f32),
        scratch_shapes=[
            pltpu.VMEM((tile_cols, waves, side, side), f32),
            pltpu.VMEM((tile_cols, waves, side, side), f32),
            pltpu.VMEM((planes * length, side), f32),
            pltpu.VMEM((3 * side, tiles * side), bf16),
            pltpu.VMEM((tiles * length, 3 * side), bf16),
            pltpu.VMEM((tiles * length, length), f32),
            pltpu.VMEM((tiles * length, length), f32),
            pltpu.VMEM((planes * length, 3 * length), bf16),
            pltpu.VMEM((3 * length, planes * side), bf16),
            pltpu.VMEM((blocks, channels, strip + side, side), f32),
            pltpu.VMEM((blocks, channels, margin, side), f32),
            pltpu.VMEM((blocks, channels, margin, side), f32),
            pltpu.VMEM((blocks, low_count, high_count, channels, slab, side), f32),
            pltpu.VMEM((blocks, low_count - 1, high_count, channels, slab, side), f32),
            pltpu.VMEM((blocks, high_count, channels, slab, side), f32),
            pltpu.VMEM((blocks, high_count - 1, channels, slab, side), f32),
            sems((2, tile_cols)),
            sems((2, tile_cols)),
            sems((2, blocks)),
            sems((2, blocks)),
            sems((blocks, low_count - 1)),
            sems((blocks, low_count - 1)),
            sems((blocks, high_count - 1)),
            sems((blocks, high_count - 1)),
        ],
        compiler_params=pltpu.CompilerParams(
            vmem_limit_bytes=VMEM_BYTES, collective_id=0, has_side_effects=True
        ),
        cost_estimate=pl.CostEstimate(
            flops=tile_cols * (tiles * 24 + planes * 36) * 2 * side**3,
            bytes_accessed=8 * waves * strip * tile_cols * side,
            transcendentals=0,
        ),
        name="camera",
    )(weights, response, *factors, scene, bank)


def per_device(scene, bank, psf_index, psf_weight, response):
    waves, tile_rows, tile_cols, side = bank.shape[:4]
    margin = side // 2
    row_ids = lax.axis_index("tile") * tile_rows + lax.iota(jnp.int32, tile_rows)[:, None, None]
    col_ids = lax.iota(jnp.int32, tile_cols)[None, :, None]
    near = 3 * (psf_index // tile_cols - row_ids + 1) + psf_index % tile_cols - col_ids + 1
    fraction = psf_weight.astype(jnp.float32) / 65536.0
    weights = jnp.sum(jnp.where(near[..., None] == lax.iota(jnp.int32, 9), fraction[..., None], 0.0), axis=2)
    own_response = lax.dynamic_slice_in_dim(response, lax.axis_index("wave") * waves, waves, 1)
    blocks = camera(
        scene, bank, weights.reshape(-1), own_response, lax.axis_size("tile"), lax.axis_size("wave")
    )
    colour = blocks.transpose(1, 2, 0, 3).reshape(blocks.shape[1], blocks.shape[2], -1)
    return colour[:, :, margin : margin + tile_cols * side]


def solution(mesh):
    in_specs = (
        P("wave", "tile", None),
        P("wave", "tile", None, None, None),
        P("tile", None, None),
        P("tile", None, None),
        P(),
    )
    out_specs = P(None, ("tile", "wave"), None)
    return jax.shard_map(
        per_device, mesh=mesh, in_specs=in_specs, out_specs=out_specs, check_vma=False
    )
```

time: 688 us -> 93.6 us (0.14)
  matrix products: 350 us -> 0 us
  waiting for transfers between devices: 202 us -> 0 us
  Pallas kernels: 0 us -> 87 us
  local copies, waits for them, and re-layouts: 74.2 us -> 3.95 us
  loops' own time: 16.7 us -> 0 us
  other arithmetic: 17.4 us -> 1.54 us
  between operations: 14.5 us -> 0.03 us
  starting transfers between devices: 9.38 us -> 0 us
    dot_general x149 -> x0, matrix products: 350 us -> none  [the longest x16 41.1 us: forward(): jnp.einsum('tkb,bl->tkl', row_imag, sin_top, precision=highest)]
    unnamed x2 -> x0, waiting for transfers between devices: 156 us -> none
    pallas_call x0 -> x1, Pallas kernels: none -> 87 us  [camera(): pl.pallas_call(functools.partial(camera_kernel, dims), grid=(blocks + 3,)...]
    ppermute x4 -> x0, waiting for transfers between devices: 45.2 us -> none  [the longest x2 22 us: from_behind(): return lax.ppermute(shard, axis, pairs)]
    dynamic_slice x36 -> x1, local copies, waits for them, and re-layouts: 23.6 us -> 0.65 us  [per_device(): lax.dynamic_slice_in_dim(response, lax.axis_index('wave') * waves, waves, 1)]
    slice x15 -> x1, local copies, waits for them, and re-layouts: 18.2 us -> 0.92 us  [per_device(): return colour[:, :, margin:margin + tile_cols * side]]
    another operation x5 -> x0, loops' own time: 16.7 us -> none  [the longest x4 10.2 us: blur_wave(): rows_out = lax.map(one_row, (scene_rows, psf_set))]
    dynamic_update_slice x12 -> x0, local copies, waits for them, and re-layouts: 13.7 us -> none  [the longest x8 8.5 us: blur_wave(): rows_out = lax.map(one_row, (scene_rows, psf_set))]
  transfers between devices with their start and end apart: 5 -> 0, of which waited for: 5 -> 0; matrix products, arithmetic and copies ran while one was open for 1% -> 0% of each run, Pallas kernels for 0% -> 0%
where the time goes in v2:
time: 93.6 us; the launch traced here: 92.5 us
  Pallas kernels  87 us (93%)
  local copies, waits for them, and re-layouts  3.95 us (4%)
  other arithmetic  1.54 us (2%)
    pallas_call x1, Pallas kernels, camera(): pl.pallas_call(functools.partial(camera_kernel, dims), grid=(blocks + 3,)...  87 us

profile of v2, /device:TPU:4, one launch (start us, length us, event | category | flops | bytes accessed | tf_op | source)
XLA Modules:
  0.0 92.5 jit_solution(1016011890532596483)
XLA Ops:
  0.0 0.0 copy-start
  0.0 0.7 copy-done
  0.7 0.6 constant_dynamic-slice_fusion.response_ref
  1.3 0.8 fusion.5
  2.1 0.7 convert_multiply_fusion
  2.8 0.1 select_reduce_fusion
  2.9 0.7 reshape.13.weight_ref
  3.5 87.0 %camera.1 = f32[9,3,32,128]{3,2,1,0:T(8,128)} custom-call(f32[144]{0:T(256)} %reshape.13.weight_ref, f32[3,4]{1,0:T(4,128)} %constant_dynamic-slice_fusion.response_ref, bf16[256,384]{1,0:T(8,128)(2,1)} %constant.59.clone.rows_in, bf16[384,256]{1,0:T(8,128)(2,1)} %constant.60.clone.cols_in, bf16[768,256]{1,0:T(8,128)(2,1)} %constant.61.clone.cols_out, ...), custom_call_target="tpu_custom_call" | custom-call | flops 13690208256 | bytes 8388608 | tf_op jit(solution)/shard_map/camera/pallas_call | solution.py:401
  90.6 1.0 %copy_bitcast_fusion = f32[3,32,1152]{2,1,0:T(8,128)S(1)} fusion(f32[9,3,32,128]{3,2,1,0:T(8,128)} %camera.1), kind=kLoop, calls=%fused_computation | loop fusion | bytes 884736 | tf_op jit(solution)/shard_map/reshape | solution.py:466
  91.6 0.9 slice.4
  (1 shorter events, 0.0 us)
Async XLA Ops:
  0.0 0.7 copy-start

commit v3 on v2

--- a/solution.py
+++ b/solution.py
@@ -58,15 +58,14 @@
     out_ref[2 * side : 3 * side, lanes] = high
 
 
-def put_cols(out_ref, values, width, rows):
+def lift(values):
     high, low = split(values)
-    out_ref[rows, 0:width] = high
-    out_ref[rows, width : 2 * width] = low
-    out_ref[rows, 2 * width : 3 * width] = high
+    return [high, low, high]
 
 
 def camera_kernel(
     dims,
+    index_ref,
     weight_ref,
     response_ref,
     rows_in,
@@ -79,8 +78,6 @@
     above,
     below,
     carry,
-    lifted,
-    lift_mid,
     scene_spec,
     psf_spec,
     mixed,
@@ -101,7 +98,7 @@
     high_sent,
     high_got,
 ):
-    tile_count, low_count, high_count, tile_rows, tile_cols, side, waves, channels = dims
+    tile_count, low_count, high_count, tile_rows, tile_cols, entries, side, waves, channels = dims
     step = pl.program_id(0)
     length, margin, strip = 2 * side, side // 2, tile_rows * side
     slab = strip // (low_count * high_count)
@@ -233,50 +230,61 @@
     def _():
         start_pair(bank_down(step + 2), bank_up(step + 2))
 
-    def transform(spec):
-        first = dot(rows_in[...], lifted[...])
-        for t in range(tile_rows * waves):
-            put_cols(lift_mid, first[:, t * side : (t + 1) * side], side, slice(t * length, (t + 1) * length))
-        spec[...] = dot(lift_mid[...], cols_in[...])
+    def transform(spec, fields):
+        tiles = tile_rows * waves
+        for t in range(0, tiles, 2):
+            pair = [jnp.concatenate(lift(field), axis=0) for field in (fields(t), fields(t + 1))]
+            first = dot(rows_in[...], jnp.concatenate(pair, axis=1))
+            pair = [jnp.concatenate(lift(first[:, j * side : (j + 1) * side]), axis=1) for j in range(2)]
+            spec[t * length : (t + 2) * length, :] = dot(jnp.concatenate(pair, axis=0), cols_in[...])
 
     @pl.when(step < tile_cols)
     def _():
+        def scene_field(t):
+            r, w = divmod(t, waves)
+            return scene_ref[w, r * side : (r + 1) * side, :]
+
+        transform(scene_spec, scene_field)
+
+        @pl.when(step == 0)
+        def _():
+            wait_pair(bank_down(0), bank_up(0))
+
+        @pl.when(step + 1 < tile_cols)
+        def _():
+            wait_pair(bank_down(step + 1), bank_up(step + 1))
+
+        near = (jnp.maximum(step - 1, 0), step, jnp.minimum(step + 1, tile_cols - 1))
+        shares = []
         for r in range(tile_rows):
-            for w in range(waves):
-                lane = (r * waves + w) * side
-                put_rows(lifted, scene_ref[w, r * side : (r + 1) * side, :], side, slice(lane, lane + side))
-        transform(scene_spec)
-
-        @pl.when(step == 0)
-        def _():
-            wait_pair(bank_down(0), bank_up(0))
-
-        @pl.when(step + 1 < tile_cols)
-        def _():
-            wait_pair(bank_down(step + 1), bank_up(step + 1))
-
-        near = (jnp.maximum(step - 1, 0), step, jnp.minimum(step + 1, tile_cols - 1))
-        for r in range(tile_rows):
-            place = (r * tile_cols + step) * 9
-            for w in range(waves):
-                psf = None
-                for i in range(3):
-                    for j in range(3):
-                        row = r + i - 1
-                        if row < 0:
-                            field = above[near[j], w]
-                        elif row >= tile_rows:
-                            field = below[near[j], w]
-                        else:
-                            field = bank_ref[w, row, near[j]]
-                        term = weight_ref[place + 3 * i + j] * field
-                        psf = term if psf is None else psf + term
-                lane = (r * waves + w) * side
-                put_rows(lifted, psf, side, slice(lane, lane + side))
-        transform(psf_spec)
-
-        def some_rows(r, index, state):
-            start = pl.multiple_of(index * CHUNK_ROWS, CHUNK_ROWS)
+            here = (tile * tile_rows + r) * tile_cols + step
+            listed = [(index_ref[r, k, step] - here, weight_ref[r, k, step]) for k in range(entries)]
+            for i in range(3):
+                for j in range(3):
+                    offset = (i - 1) * tile_cols + j - 1
+                    share = sum(jnp.where(away == offset, weight, 0) for away, weight in listed)
+                    shares.append(share.astype(jnp.float32) * (1.0 / 65536.0))
+
+        def psf_field(t):
+            r, w = divmod(t, waves)
+            psf = None
+            for i in range(3):
+                for j in range(3):
+                    row = r + i - 1
+                    if row < 0:
+                        field = above[near[j], w]
+                    elif row >= tile_rows:
+                        field = below[near[j], w]
+                    else:
+                        field = bank_ref[w, row, near[j]]
+                    term = shares[9 * r + 3 * i + j] * field
+                    psf = term if psf is None else psf + term
+            return psf
+
+        transform(psf_spec, psf_field)
+
+        def some_rows(r, index):
+            start = index * CHUNK_ROWS
             left, right = slice(0, side), slice(side, length)
             sums = [None] * channels
             for w in range(waves):
@@ -295,7 +303,7 @@
                 q2r, q2i = s2r * p2r - s2i * p2i, s2r * p2i + s2i * p2r
                 parts = (q1r + q2r, q2i - q1i, q1i + q2i, q1r - q2r)
                 for ch in range(channels):
-                    gain = response_ref[ch, w]
+                    gain = response_ref[ch, wave * waves + w]
                     terms = [gain * value for value in parts]
                     sums[ch] = terms if w == 0 else [old + new for old, new in zip(sums[ch], terms)]
             for ch in range(channels):
@@ -306,10 +314,10 @@
                         mixed[rows, h * side : (h + 1) * side] = upper_bits
                         mixed[rows, length + h * side : length + (h + 1) * side] = lower_bits
                         mixed[rows, 2 * length + h * side : 2 * length + (h + 1) * side] = upper_bits
-            return state
 
         for r in range(tile_rows):
-            lax.fori_loop(0, side // CHUNK_ROWS, functools.partial(some_rows, r), 0)
+            for index in range(side // CHUNK_ROWS):
+                some_rows(r, index)
         partial = dot(mixed[...], cols_out[...])
         for r in range(tile_rows):
             for ch in range(channels):
@@ -380,19 +388,20 @@
         total = part[b, high]
         for d in range(1, high_count):
             total = total + got_high[b, d - 1]
-        out_ref[b] = total
-
-
-def camera(scene, bank, weights, response, tile_count, wave_count):
+        out_ref[:, :, pl.ds(pl.multiple_of(b * side, side), side)] = total
+
+
+def camera(scene, bank, index, weights, response, tile_count, wave_count):
     waves, tile_rows, tile_cols, side = bank.shape[:4]
     channels = response.shape[0]
     length, strip, margin = 2 * side, tile_rows * side, side // 2
+    entries = index.shape[1]
     blocks = tile_cols + 1
     low_count = 1 << ((wave_count.bit_length() - 1) // 2)
     high_count = wave_count // low_count
     slab = strip // wave_count
     factors = tables(side)
-    dims = (tile_count, low_count, high_count, tile_rows, tile_cols, side, waves, channels)
+    dims = (tile_count, low_count, high_count, tile_rows, tile_cols, entries, side, waves, channels)
     smem = pl.BlockSpec(memory_space=pltpu.SMEM)
     vmem = pl.BlockSpec(memory_space=pltpu.VMEM)
     f32, bf16, sems = jnp.float32, jnp.bfloat16, pltpu.SemaphoreType.DMA
@@ -404,6 +413,7 @@
         in_specs=[
             smem,
             smem,
+            smem,
             vmem,
             vmem,
             vmem,
@@ -412,13 +422,11 @@
             vmem,
         ],
         out_specs=vmem,
-        out_shape=jax.ShapeDtypeStruct((blocks, channels, slab, side), f32),
+        out_shape=jax.ShapeDtypeStruct((channels, slab, blocks * side), f32),
         scratch_shapes=[
             pltpu.VMEM((tile_cols, waves, side, side), f32),
             pltpu.VMEM((tile_cols, waves, side, side), f32),
             pltpu.VMEM((planes * length, side), f32),
-            pltpu.VMEM((3 * side, tiles * side), bf16),
-            pltpu.VMEM((tiles * length, 3 * side), bf16),
             pltpu.VMEM((tiles * length, length), f32),
             pltpu.VMEM((tiles * length, length), f32),
             pltpu.VMEM((planes * length, 3 * length), bf16),
@@ -448,22 +456,21 @@
             transcendentals=0,
         ),
         name="camera",
-    )(weights, response, *factors, scene, bank)
+    )(index, weights, response, *factors, scene, bank)
 
 
 def per_device(scene, bank, psf_index, psf_weight, response):
-    waves, tile_rows, tile_cols, side = bank.shape[:4]
+    tile_cols, side = bank.shape[2:4]
     margin = side // 2
-    row_ids = lax.axis_index("tile") * tile_rows + lax.iota(jnp.int32, tile_rows)[:, None, None]
-    col_ids = lax.iota(jnp.int32, tile_cols)[None, :, None]
-    near = 3 * (psf_index // tile_cols - row_ids + 1) + psf_index % tile_cols - col_ids + 1
-    fraction = psf_weight.astype(jnp.float32) / 65536.0
-    weights = jnp.sum(jnp.where(near[..., None] == lax.iota(jnp.int32, 9), fraction[..., None], 0.0), axis=2)
-    own_response = lax.dynamic_slice_in_dim(response, lax.axis_index("wave") * waves, waves, 1)
-    blocks = camera(
-        scene, bank, weights.reshape(-1), own_response, lax.axis_size("tile"), lax.axis_size("wave")
+    colour = camera(
+        scene,
+        bank,
+        psf_index.transpose(0, 2, 1),
+        psf_weight.transpose(0, 2, 1),
+        response,
+        lax.axis_size("tile"),
+        lax.axis_size("wave"),
     )
-    colour = blocks.transpose(1, 2, 0, 3).reshape(blocks.shape[1], blocks.shape[2], -1)
     return colour[:, :, margin : margin + tile_cols * side]
 
 

time: 93.6 us -> 79.3 us (0.85); the launches traced: 92.5 us -> 79.2 us
  Pallas kernels: 87 us -> 77.3 us
  local copies, waits for them, and re-layouts: 3.95 us -> 1.93 us
  other arithmetic: 1.54 us -> 0 us
    pallas_call x1, Pallas kernels: 87 us -> 77.3 us  [camera(): pl.pallas_call(functools.partial(camera_kernel, dims), grid=(blocks + 3,)...]
    reshape x2 -> x0, local copies, waits for them, and re-layouts: 1.71 us -> none  [the longest x1 1.04 us: per_device(): blocks.transpose(1, 2, 0, 3).reshape(blocks.shape[1], blocks.shape[2], -1)]
    slice x1, local copies, waits for them, and re-layouts: 0.92 us -> 1.93 us  [per_device(): return colour[:, :, margin:margin + tile_cols * side]]
where the time goes in v3:
time: 79.3 us; the launch traced here: 79.2 us
  Pallas kernels  77.3 us (97%)
  local copies, waits for them, and re-layouts  1.93 us (2%)
    pallas_call x1, Pallas kernels, camera(): pl.pallas_call(functools.partial(camera_kernel, dims), grid=(blocks + 3,)...  77.3 us
    slice x1, local copies, waits for them, and re-layouts, per_device(): return colour[:, :, margin:margin + tile_cols * side]  1.93 us

profile of v3, /device:TPU:4, one launch (start us, length us, event | category | flops | bytes accessed | tf_op | source)
XLA Modules:
  0.0 79.2 jit_solution(11139587578599775220)
XLA Ops:
  0.0 77.3 %camera.1 = f32[3,32,1152]{2,1,0:T(8,128)} custom-call(s32[2,4,8]{2,1,0:T(4,128)} %bitcast.2, s32[2,4,8]{2,1,0:T(4,128)} %bitcast.3, f32[3,32]{1,0:T(4,128)} %response_ref.1, bf16[256,384]{1,0:T(8,128)(2,1)} %constant.8.clone.rows_in, bf16[384,256]{1,0:T(8,128)(2,1)} %constant.9.clone.cols_in, bf16[768,256]{1,0:T(8,128)(2,1)} %constant.10.clone.cols_out, ...), custom_call_target="tpu_custom_call" | custom-call | flops 13690208256 | bytes 8388608 | tf_op jit(solution)/shard_map/camera/pallas_call | solution.py:410
  77.3 1.9 %slice.3 = f32[3,32,1024]{2,1,0:T(8,128)} slice(f32[3,32,1152]{2,1,0:T(8,128)} %camera.1), slice={[0:3], [0:32], [64:1088]} | slice | bytes 786432 | tf_op jit(solution)/shard_map/slice | solution.py:474

commit v4 on v3

--- a/solution.py
+++ b/solution.py
@@ -78,10 +78,12 @@
     above,
     below,
     carry,
+    scene_next,
     scene_spec,
     psf_spec,
     mixed,
     back,
+    last,
     light,
     light_above,
     light_below,
@@ -212,7 +214,7 @@
 
         others = low_count + high_count - 2
         pl.semaphore_wait(barrier, others + has_above.astype(jnp.int32) + has_below.astype(jnp.int32))
-        for c in range(min(3, tile_cols)):
+        for c in range(2):
             start_pair(bank_down(c), bank_up(c))
         carry[...] = jnp.zeros_like(carry)
 
@@ -226,39 +228,43 @@
             below[...] = jnp.zeros_like(below)
             light_below[...] = jnp.zeros_like(light_below)
 
-    @pl.when(jnp.logical_and(step > 0, step + 2 < tile_cols))
-    def _():
-        start_pair(bank_down(step + 2), bank_up(step + 2))
-
-    def transform(spec, fields):
-        tiles = tile_rows * waves
+    def transform(spec, fields, t):
+        pair = [jnp.concatenate(lift(field), axis=0) for field in (fields(t), fields(t + 1))]
+        first = dot(rows_in[...], jnp.concatenate(pair, axis=1))
+        pair = [jnp.concatenate(lift(first[:, j * side : (j + 1) * side]), axis=1) for j in range(2)]
+        spec[t * length : (t + 2) * length, :] = dot(jnp.concatenate(pair, axis=0), cols_in[...])
+
+    def scene_field(t):
+        r, w = divmod(t, waves)
+        return scene_ref[w, r * side : (r + 1) * side, :]
+
+    tiles = tile_rows * waves
+
+    @pl.when(step == 0)
+    def _():
         for t in range(0, tiles, 2):
-            pair = [jnp.concatenate(lift(field), axis=0) for field in (fields(t), fields(t + 1))]
-            first = dot(rows_in[...], jnp.concatenate(pair, axis=1))
-            pair = [jnp.concatenate(lift(first[:, j * side : (j + 1) * side]), axis=1) for j in range(2)]
-            spec[t * length : (t + 2) * length, :] = dot(jnp.concatenate(pair, axis=0), cols_in[...])
-
-    @pl.when(step < tile_cols)
-    def _():
-        def scene_field(t):
-            r, w = divmod(t, waves)
-            return scene_ref[w, r * side : (r + 1) * side, :]
-
-        transform(scene_spec, scene_field)
-
-        @pl.when(step == 0)
-        def _():
-            wait_pair(bank_down(0), bank_up(0))
+            transform(scene_next, scene_field, t)
+
+    @pl.when(step == 1)
+    def _():
+        wait_pair(bank_down(0), bank_up(0))
+
+    @pl.when(jnp.logical_and(step >= 1, step < tile_cols))
+    def _():
+        wait_pair(bank_down(step), bank_up(step))
 
         @pl.when(step + 1 < tile_cols)
         def _():
-            wait_pair(bank_down(step + 1), bank_up(step + 1))
-
-        near = (jnp.maximum(step - 1, 0), step, jnp.minimum(step + 1, tile_cols - 1))
+            start_pair(bank_down(step + 1), bank_up(step + 1))
+
+    @pl.when(jnp.logical_and(step >= 1, step <= tile_cols))
+    def _():
+        col = step - 1
+        near = (jnp.maximum(col - 1, 0), col, jnp.minimum(col + 1, tile_cols - 1))
         shares = []
         for r in range(tile_rows):
-            here = (tile * tile_rows + r) * tile_cols + step
-            listed = [(index_ref[r, k, step] - here, weight_ref[r, k, step]) for k in range(entries)]
+            here = (tile * tile_rows + r) * tile_cols + col
+            listed = [(index_ref[r, k, col] - here, weight_ref[r, k, col]) for k in range(entries)]
             for i in range(3):
                 for j in range(3):
                     offset = (i - 1) * tile_cols + j - 1
@@ -281,7 +287,20 @@
                     psf = term if psf is None else psf + term
             return psf
 
-        transform(psf_spec, psf_field)
+        for t in range(tiles):
+            top = t * length
+            upper, lower = slice(top, top + side), slice(top + side, top + length)
+            left, right = slice(0, side), slice(side, length)
+            a, b, d, e = (
+                scene_next[upper, left],
+                scene_next[upper, right],
+                scene_next[lower, left],
+                scene_next[lower, right],
+            )
+            scene_spec[upper, left], scene_spec[lower, left] = a + e, d - b
+            scene_spec[upper, right], scene_spec[lower, right] = a - e, d + b
+            if t % 2 == 1:
+                transform(psf_spec, psf_field, t - 1)
 
         def some_rows(r, index):
             start = index * CHUNK_ROWS
@@ -292,13 +311,8 @@
                 lower = pl.ds(start + (r * waves + w) * length + side, CHUNK_ROWS)
                 a, b, d, e = psf_spec[upper, left], psf_spec[upper, right], psf_spec[lower, left], psf_spec[lower, right]
                 p1r, p1i, p2r, p2i = a + e, d - b, a - e, d + b
-                a, b, d, e = (
-                    scene_spec[upper, left],
-                    scene_spec[upper, right],
-                    scene_spec[lower, left],
-                    scene_spec[lower, right],
-                )
-                s1r, s1i, s2r, s2i = a + e, d - b, a - e, d + b
+                s1r, s1i = scene_spec[upper, left], scene_spec[lower, left]
+                s2r, s2i = scene_spec[upper, right], scene_spec[lower, right]
                 q1r, q1i = s1r * p1r - s1i * p1i, s1r * p1i + s1i * p1r
                 q2r, q2i = s2r * p2r - s2i * p2i, s2r * p2i + s2i * p2r
                 parts = (q1r + q2r, q2i - q1i, q1i + q2i, q1r - q2r)
@@ -315,18 +329,24 @@
                         mixed[rows, length + h * side : length + (h + 1) * side] = lower_bits
                         mixed[rows, 2 * length + h * side : 2 * length + (h + 1) * side] = upper_bits
 
+        ahead = list(range(0, tiles, 2))
+        chunks = side // CHUNK_ROWS
+        every = max(1, tile_rows * chunks // len(ahead))
         for r in range(tile_rows):
-            for index in range(side // CHUNK_ROWS):
+            for index in range(chunks):
                 some_rows(r, index)
-        partial = dot(mixed[...], cols_out[...])
-        for r in range(tile_rows):
+                if (r * chunks + index + 1) % every == every // 2 and ahead:
+                    transform(scene_next, scene_field, ahead.pop(0))
+            planes = slice(r * channels * length, (r + 1) * channels * length)
+            partial = dot(mixed[planes, :], cols_out[...])
             for ch in range(channels):
                 rows = slice((r * channels + ch) * length, (r * channels + ch + 1) * length)
                 lane = (r * channels + ch) * side
-                put_rows(back, partial[rows, 0:side] + carry[rows, :], length, slice(lane, lane + side))
-                carry[rows, :] = partial[rows, side:length]
-
-    @pl.when(step == tile_cols)
+                block = partial[ch * length : (ch + 1) * length, :]
+                put_rows(back, block[:, 0:side] + carry[rows, :], length, slice(lane, lane + side))
+                carry[rows, :] = block[:, side:length]
+
+    @pl.when(step == tile_cols + 1)
     def _():
         for r in range(tile_rows):
             for ch in range(channels):
@@ -334,8 +354,9 @@
                 lane = (r * channels + ch) * side
                 put_rows(back, carry[rows, :], length, slice(lane, lane + side))
 
-    @pl.when(step < blocks)
-    def _():
+    @pl.when(jnp.logical_and(step >= 1, step <= blocks))
+    def _():
+        now = step - 1
         rays = dot(rows_out[...], back[...])
         for ch in range(channels):
             for r in range(tile_rows + 1):
@@ -347,12 +368,12 @@
                     lane = ((r - 1) * channels + ch) * side
                     tail = rays[side:length, lane : lane + side]
                     total = tail if total is None else total + tail
-                light[step, ch, r * side : (r + 1) * side, :] = total
-        start_pair(light_down(step), light_up(step))
-
-    @pl.when(jnp.logical_and(step >= 1, step < blocks + 1))
-    def _():
-        b = step - 1
+                light[now, ch, r * side : (r + 1) * side, :] = total
+        start_pair(light_down(now), light_up(now))
+
+    @pl.when(jnp.logical_and(step >= 2, step < blocks + 2))
+    def _():
+        b = step - 2
         wait_pair(light_down(b), light_up(b))
         for ch in range(channels):
             for h in range(high_count):
@@ -368,9 +389,9 @@
         for d in range(1, low_count):
             to_low(b, d).start()
 
-    @pl.when(jnp.logical_and(step >= 2, step < blocks + 2))
-    def _():
-        b = step - 2
+    @pl.when(jnp.logical_and(step >= 3, step < blocks + 3))
+    def _():
+        b = step - 3
         for d in range(1, low_count):
             to_low(b, d).wait()
         total = middle[b, low]
@@ -380,15 +401,23 @@
         for d in range(1, high_count):
             to_high(b, d).start()
 
-    @pl.when(step >= 3)
-    def _():
-        b = step - 3
+    @pl.when(step >= 4)
+    def _():
+        b = step - 4
         for d in range(1, high_count):
             to_high(b, d).wait()
         total = part[b, high]
         for d in range(1, high_count):
             total = total + got_high[b, d - 1]
-        out_ref[:, :, pl.ds(pl.multiple_of(b * side, side), side)] = total
+        turned = pltpu.roll(total.reshape(channels * slab, side), margin, 1)
+
+        @pl.when(b > 0)
+        def _():
+            is_left = lax.broadcasted_iota(jnp.int32, turned.shape, 1) < margin
+            whole = jnp.where(is_left, last[...], turned).reshape(channels, slab, side)
+            out_ref[:, :, pl.ds(pl.multiple_of((b - 1) * side, side), side)] = whole
+
+        last[...] = turned
 
 
 def camera(scene, bank, index, weights, response, tile_count, wave_count):
@@ -409,7 +438,7 @@
     planes = tile_rows * channels
     return pl.pallas_call(
         functools.partial(camera_kernel, dims),
-        grid=(blocks + 3,),
+        grid=(blocks + 4,),
         in_specs=[
             smem,
             smem,
@@ -422,15 +451,17 @@
             vmem,
         ],
         out_specs=vmem,
-        out_shape=jax.ShapeDtypeStruct((channels, slab, blocks * side), f32),
+        out_shape=jax.ShapeDtypeStruct((channels, slab, tile_cols * side), f32),
         scratch_shapes=[
             pltpu.VMEM((tile_cols, waves, side, side), f32),
             pltpu.VMEM((tile_cols, waves, side, side), f32),
             pltpu.VMEM((planes * length, side), f32),
             pltpu.VMEM((tiles * length, length), f32),
             pltpu.VMEM((tiles * length, length), f32),
+            pltpu.VMEM((tiles * length, length), f32),
             pltpu.VMEM((planes * length, 3 * length), bf16),
             pltpu.VMEM((3 * length, planes * side), bf16),
+            pltpu.VMEM((channels * slab, side), f32),
             pltpu.VMEM((blocks, channels, strip + side, side), f32),
             pltpu.VMEM((blocks, channels, margin, side), f32),
             pltpu.VMEM((blocks, channels, margin, side), f32),
@@ -460,9 +491,7 @@
 
 
 def per_device(scene, bank, psf_index, psf_weight, response):
-    tile_cols, side = bank.shape[2:4]
-    margin = side // 2
-    colour = camera(
+    return camera(
         scene,
         bank,
         psf_index.transpose(0, 2, 1),
@@ -471,7 +500,6 @@
         lax.axis_size("tile"),
         lax.axis_size("wave"),
     )
-    return colour[:, :, margin : margin + tile_cols * side]
 
 
 def solution(mesh):

time: 79.3 us -> 79.6 us (level)
    slice x1 -> x0, local copies, waits for them, and re-layouts: 1.93 us -> none  [per_device(): return colour[:, :, margin:margin + tile_cols * side]]
    unnamed x0 -> x1, local copies, waits for them, and re-layouts: none -> 1.77 us
where the time goes in v4:
time: 79.6 us; the launch traced here: 79.4 us
  Pallas kernels  77.6 us (97%)
  local copies, waits for them, and re-layouts  1.77 us (2%)
    pallas_call x1, Pallas kernels, camera(): pl.pallas_call(functools.partial(camera_kernel, dims), grid=(blocks + 4,)...  77.6 us
    unnamed x1, local copies, waits for them, and re-layouts  1.77 us

profile of v4, /device:TPU:4, one launch (start us, length us, event | category | flops | bytes accessed | tf_op | source)
XLA Modules:
  0.0 79.4 jit_solution(14085437916291120145)
XLA Ops:
  0.0 77.6 %camera.1 = f32[3,32,1024]{2,1,0:T(8,128)} custom-call(s32[2,4,8]{2,1,0:T(4,128)} %bitcast.2, s32[2,4,8]{2,1,0:T(4,128)} %bitcast.3, f32[3,32]{1,0:T(4,128)} %response_ref.1, bf16[256,384]{1,0:T(8,128)(2,1)} %constant.8.clone.rows_in, bf16[384,256]{1,0:T(8,128)(2,1)} %constant.9.clone.cols_in, bf16[768,256]{1,0:T(8,128)(2,1)} %constant.10.clone.cols_out, ...), custom_call_target="tpu_custom_call" | custom-call | flops 13690208256 | bytes 8388608 | tf_op jit(solution)/shard_map/camera/pallas_call | solution.py:439
  77.7 1.8 %copy.11 = f32[3,32,1024]{2,1,0:T(8,128)} copy(f32[3,32,1024]{2,1,0:T(8,128)} %camera.1) | data formatting | bytes 786432

commit v5 on v4

--- a/solution.py
+++ b/solution.py
@@ -78,9 +78,8 @@
     above,
     below,
     carry,
-    scene_next,
-    scene_spec,
-    psf_spec,
+    scene_mid,
+    psf_mid,
     mixed,
     back,
     last,
@@ -228,11 +227,14 @@
             below[...] = jnp.zeros_like(below)
             light_below[...] = jnp.zeros_like(light_below)
 
-    def transform(spec, fields, t):
+    def transform_rows(mid, fields, t):
         pair = [jnp.concatenate(lift(field), axis=0) for field in (fields(t), fields(t + 1))]
         first = dot(rows_in[...], jnp.concatenate(pair, axis=1))
-        pair = [jnp.concatenate(lift(first[:, j * side : (j + 1) * side]), axis=1) for j in range(2)]
-        spec[t * length : (t + 2) * length, :] = dot(jnp.concatenate(pair, axis=0), cols_in[...])
+        for j in range(2):
+            upper_bits, lower_bits = split(first[:, j * side : (j + 1) * side])
+            rows = slice((t + j) * length, (t + j + 1) * length)
+            mid[rows, 0:side] = upper_bits
+            mid[rows, side:length] = lower_bits
 
     def scene_field(t):
         r, w = divmod(t, waves)
@@ -240,26 +242,24 @@
 
     tiles = tile_rows * waves
 
-    @pl.when(step == 0)
-    def _():
+    @pl.when(step < tile_cols)
+    def _():
+        col = step
         for t in range(0, tiles, 2):
-            transform(scene_next, scene_field, t)
-
-    @pl.when(step == 1)
-    def _():
-        wait_pair(bank_down(0), bank_up(0))
-
-    @pl.when(jnp.logical_and(step >= 1, step < tile_cols))
-    def _():
-        wait_pair(bank_down(step), bank_up(step))
+            transform_rows(scene_mid, scene_field, t)
+
+        @pl.when(step == 0)
+        def _():
+            wait_pair(bank_down(0), bank_up(0))
 
         @pl.when(step + 1 < tile_cols)
         def _():
-            start_pair(bank_down(step + 1), bank_up(step + 1))
-
-    @pl.when(jnp.logical_and(step >= 1, step <= tile_cols))
-    def _():
-        col = step - 1
+            wait_pair(bank_down(step + 1), bank_up(step + 1))
+
+        @pl.when(step + 2 < tile_cols)
+        def _():
+            start_pair(bank_down(step + 2), bank_up(step + 2))
+
         near = (jnp.maximum(col - 1, 0), col, jnp.minimum(col + 1, tile_cols - 1))
         shares = []
         for r in range(tile_rows):
@@ -287,32 +287,30 @@
                     psf = term if psf is None else psf + term
             return psf
 
-        for t in range(tiles):
-            top = t * length
-            upper, lower = slice(top, top + side), slice(top + side, top + length)
-            left, right = slice(0, side), slice(side, length)
-            a, b, d, e = (
-                scene_next[upper, left],
-                scene_next[upper, right],
-                scene_next[lower, left],
-                scene_next[lower, right],
-            )
-            scene_spec[upper, left], scene_spec[lower, left] = a + e, d - b
-            scene_spec[upper, right], scene_spec[lower, right] = a - e, d + b
-            if t % 2 == 1:
-                transform(psf_spec, psf_field, t - 1)
+        for t in range(0, tiles, 2):
+            transform_rows(psf_mid, psf_field, t)
 
         def some_rows(r, index):
             start = index * CHUNK_ROWS
-            left, right = slice(0, side), slice(side, length)
+            lines = []
+            for w in range(waves):
+                top = start + (r * waves + w) * length
+                for mid in (scene_mid, psf_mid):
+                    for first in (top, top + side):
+                        both = mid[first : first + CHUNK_ROWS, :]
+                        lines.append(jnp.concatenate([both, both[:, 0:side]], axis=1))
+            spec = dot(jnp.concatenate(lines, axis=0), cols_in[...])
+
+            def quarters(block):
+                top = block * 2 * CHUNK_ROWS
+                upper, lower = slice(top, top + CHUNK_ROWS), slice(top + CHUNK_ROWS, top + 2 * CHUNK_ROWS)
+                a, b, d, e = spec[upper, :side], spec[upper, side:], spec[lower, :side], spec[lower, side:]
+                return a + e, d - b, a - e, d + b
+
             sums = [None] * channels
             for w in range(waves):
-                upper = pl.ds(start + (r * waves + w) * length, CHUNK_ROWS)
-                lower = pl.ds(start + (r * waves + w) * length + side, CHUNK_ROWS)
-                a, b, d, e = psf_spec[upper, left], psf_spec[upper, right], psf_spec[lower, left], psf_spec[lower, right]
-                p1r, p1i, p2r, p2i = a + e, d - b, a - e, d + b
-                s1r, s1i = scene_spec[upper, left], scene_spec[lower, left]
-                s2r, s2i = scene_spec[upper, right], scene_spec[lower, right]
+                s1r, s1i, s2r, s2i = quarters(2 * w)
+                p1r, p1i, p2r, p2i = quarters(2 * w + 1)
                 q1r, q1i = s1r * p1r - s1i * p1i, s1r * p1i + s1i * p1r
                 q2r, q2i = s2r * p2r - s2i * p2i, s2r * p2i + s2i * p2r
                 parts = (q1r + q2r, q2i - q1i, q1i + q2i, q1r - q2r)
@@ -329,14 +327,9 @@
                         mixed[rows, length + h * side : length + (h + 1) * side] = lower_bits
                         mixed[rows, 2 * length + h * side : 2 * length + (h + 1) * side] = upper_bits
 
-        ahead = list(range(0, tiles, 2))
-        chunks = side // CHUNK_ROWS
-        every = max(1, tile_rows * chunks // len(ahead))
         for r in range(tile_rows):
-            for index in range(chunks):
+            for index in range(side // CHUNK_ROWS):
                 some_rows(r, index)
-                if (r * chunks + index + 1) % every == every // 2 and ahead:
-                    transform(scene_next, scene_field, ahead.pop(0))
             planes = slice(r * channels * length, (r + 1) * channels * length)
             partial = dot(mixed[planes, :], cols_out[...])
             for ch in range(channels):
@@ -346,7 +339,7 @@
                 put_rows(back, block[:, 0:side] + carry[rows, :], length, slice(lane, lane + side))
                 carry[rows, :] = block[:, side:length]
 
-    @pl.when(step == tile_cols + 1)
+    @pl.when(step == tile_cols)
     def _():
         for r in range(tile_rows):
             for ch in range(channels):
@@ -354,9 +347,9 @@
                 lane = (r * channels + ch) * side
                 put_rows(back, carry[rows, :], length, slice(lane, lane + side))
 
-    @pl.when(jnp.logical_and(step >= 1, step <= blocks))
-    def _():
-        now = step - 1
+    @pl.when(step < blocks)
+    def _():
+        now = step
         rays = dot(rows_out[...], back[...])
         for ch in range(channels):
             for r in range(tile_rows + 1):
@@ -371,9 +364,9 @@
                 light[now, ch, r * side : (r + 1) * side, :] = total
         start_pair(light_down(now), light_up(now))
 
-    @pl.when(jnp.logical_and(step >= 2, step < blocks + 2))
-    def _():
-        b = step - 2
+    @pl.when(jnp.logical_and(step >= 1, step < blocks + 1))
+    def _():
+        b = step - 1
         wait_pair(light_down(b), light_up(b))
         for ch in range(channels):
             for h in range(high_count):
@@ -389,9 +382,9 @@
         for d in range(1, low_count):
             to_low(b, d).start()
 
-    @pl.when(jnp.logical_and(step >= 3, step < blocks + 3))
-    def _():
-        b = step - 3
+    @pl.when(jnp.logical_and(step >= 2, step < blocks + 2))
+    def _():
+        b = step - 2
         for d in range(1, low_count):
             to_low(b, d).wait()
         total = middle[b, low]
@@ -401,9 +394,9 @@
         for d in range(1, high_count):
             to_high(b, d).start()
 
-    @pl.when(step >= 4)
-    def _():
-        b = step - 4
+    @pl.when(step >= 3)
+    def _():
+        b = step - 3
         for d in range(1, high_count):
             to_high(b, d).wait()
         total = part[b, high]
@@ -438,7 +431,7 @@
     planes = tile_rows * channels
     return pl.pallas_call(
         functools.partial(camera_kernel, dims),
-        grid=(blocks + 4,),
+        grid=(blocks + 3,),
         in_specs=[
             smem,
             smem,
@@ -456,9 +449,8 @@
             pltpu.VMEM((tile_cols, waves, side, side), f32),
             pltpu.VMEM((tile_cols, waves, side, side), f32),
             pltpu.VMEM((planes * length, side), f32),
-            pltpu.VMEM((tiles * length, length), f32),
-            pltpu.VMEM((tiles * length, length), f32),
-            pltpu.VMEM((tiles * length, length), f32),
+            pltpu.VMEM((tiles * length, length), bf16),
+            pltpu.VMEM((tiles * length, length), bf16),
             pltpu.VMEM((planes * length, 3 * length), bf16),
             pltpu.VMEM((3 * length, planes * side), bf16),
             pltpu.VMEM((channels * slab, side), f32),

time: 79.6 us -> 78.6 us (0.987)
  Pallas kernels: 77.6 us -> 76.6 us
    pallas_call x1, Pallas kernels: 77.6 us -> 76.6 us  [camera(): pl.pallas_call(functools.partial(camera_kernel, dims), grid=(blocks + 3,)...]
where the time goes in v5:
time: 78.6 us; the launch traced here: 78.4 us
  Pallas kernels  76.6 us (97%)
  local copies, waits for them, and re-layouts  1.77 us (2%)
    pallas_call x1, Pallas kernels, camera(): pl.pallas_call(functools.partial(camera_kernel, dims), grid=(blocks + 3,)...  76.6 us
    unnamed x1, local copies, waits for them, and re-layouts  1.77 us

profile of v5, /device:TPU:4, one launch (start us, length us, event | category | flops | bytes accessed | tf_op | source)
XLA Modules:
  0.0 78.4 jit_solution(1077236299659053713)
XLA Ops:
  0.0 76.6 %camera.1 = f32[3,32,1024]{2,1,0:T(8,128)} custom-call(s32[2,4,8]{2,1,0:T(4,128)} %bitcast.2, s32[2,4,8]{2,1,0:T(4,128)} %bitcast.3, f32[3,32]{1,0:T(4,128)} %response_ref.1, bf16[256,384]{1,0:T(8,128)(2,1)} %constant.8.clone.rows_in, bf16[384,256]{1,0:T(8,128)(2,1)} %constant.9.clone.cols_in, bf16[768,256]{1,0:T(8,128)(2,1)} %constant.10.clone.cols_out, ...), custom_call_target="tpu_custom_call" | custom-call | flops 13690208256 | bytes 8388608 | tf_op jit(solution)/shard_map/camera/pallas_call | solution.py:432
  76.6 1.8 %copy.11 = f32[3,32,1024]{2,1,0:T(8,128)} copy(f32[3,32,1024]{2,1,0:T(8,128)} %camera.1) | data formatting | bytes 786432

commit v6 on v5

--- a/solution.py
+++ b/solution.py
@@ -75,6 +75,7 @@
     scene_ref,
     bank_ref,
     out_ref,
+    own,
     above,
     below,
     carry,
@@ -90,6 +91,7 @@
     got_low,
     part,
     got_high,
+    bank_held,
     bank_sent,
     bank_got,
     light_sent,
@@ -104,6 +106,9 @@
     length, margin, strip = 2 * side, side // 2, tile_rows * side
     slab = strip // (low_count * high_count)
     blocks = tile_cols + 1
+    edge = margin * high_count // strip
+    inner, outer = range(edge, high_count - edge), [*range(edge), *range(high_count - edge, high_count)]
+    spans = ((edge, high_count - 2 * edge), (0, edge), (high_count - edge, edge))
     tile, wave = lax.axis_index("tile"), lax.axis_index("wave")
     low, high = lax.rem(wave, low_count), lax.div(wave, low_count)
     has_above, has_below = tile > 0, tile < tile_count - 1
@@ -120,6 +125,9 @@
             device_id_type=pl.DeviceIdType.MESH,
         )
 
+    def bank_own(c):
+        return pltpu.make_async_copy(bank_ref.at[:, :, c], own.at[:, :, c], bank_held.at[c])
+
     def bank_down(c):
         return remote(
             bank_ref.at[:, tile_rows - 1, c], above.at[c], bank_sent.at[0, c], bank_got.at[0, c], "tile", tile_below
@@ -169,16 +177,50 @@
     def high_peer(d):
         return lax.rem(high + d, high_count)
 
-    def to_low(b, d):
+    def to_low(b, d, part_id):
         peer = low_peer(d)
+        first, count = spans[part_id]
         return remote(
-            middle.at[b, peer],
-            got_low.at[b, d - 1],
-            low_sent.at[b, d - 1],
-            low_got.at[b, d - 1],
+            middle.at[b, peer, pl.ds(first, count)],
+            got_low.at[b, d - 1, pl.ds(first, count)],
+            low_sent.at[b, d - 1, part_id],
+            low_got.at[b, d - 1, part_id],
             "wave",
             high * low_count + peer,
         )
+
+    def send_slabs(b, slabs, part_ids):
+        for ch in range(channels):
+            for h in slabs:
+                for o in range(low_count):
+                    start = (h * low_count + o) * slab
+                    value = light[b, ch, margin + start : margin + start + slab, :]
+                    if start < margin:
+                        value = value + light_above[b, ch, start : start + slab, :]
+                    if start >= strip - margin:
+                        start = start - (strip - margin)
+                        value = value + light_below[b, ch, start : start + slab, :]
+                    middle[b, o, h, ch] = value
+        for d in range(1, low_count):
+            for part_id in part_ids:
+                to_low(b, d, part_id).start()
+
+    def sum_slabs(b, slabs, part_ids):
+        for d in range(1, low_count):
+            for part_id in part_ids:
+                to_low(b, d, part_id).wait()
+        for h in slabs:
+            total = middle[b, low, h]
+            for d in range(1, low_count):
+                total = total + got_low[b, d - 1, h]
+            part[b, h] = total
+        for d in range(1, high_count):
+            peer = high_peer(d)
+            is_inner = jnp.logical_and(peer >= edge, peer < high_count - edge)
+
+            @pl.when(is_inner if slabs is inner else jnp.logical_not(is_inner))
+            def _():
+                to_high(b, d).start()
 
     def to_high(b, d):
         peer = high_peer(d)
@@ -215,6 +257,8 @@
         pl.semaphore_wait(barrier, others + has_above.astype(jnp.int32) + has_below.astype(jnp.int32))
         for c in range(2):
             start_pair(bank_down(c), bank_up(c))
+        for c in range(tile_cols):
+            bank_own(c).start()
         carry[...] = jnp.zeros_like(carry)
 
         @pl.when(jnp.logical_not(has_above))
@@ -250,10 +294,12 @@
 
         @pl.when(step == 0)
         def _():
+            bank_own(0).wait()
             wait_pair(bank_down(0), bank_up(0))
 
         @pl.when(step + 1 < tile_cols)
         def _():
+            bank_own(step + 1).wait()
             wait_pair(bank_down(step + 1), bank_up(step + 1))
 
         @pl.when(step + 2 < tile_cols)
@@ -282,7 +328,7 @@
                     elif row >= tile_rows:
                         field = below[near[j], w]
                     else:
-                        field = bank_ref[w, row, near[j]]
+                        field = own[w, row, near[j]]
                     term = shares[9 * r + 3 * i + j] * field
                     psf = term if psf is None else psf + term
             return psf
@@ -363,36 +409,18 @@
                     total = tail if total is None else total + tail
                 light[now, ch, r * side : (r + 1) * side, :] = total
         start_pair(light_down(now), light_up(now))
+        send_slabs(now, inner, (0,))
 
     @pl.when(jnp.logical_and(step >= 1, step < blocks + 1))
     def _():
         b = step - 1
         wait_pair(light_down(b), light_up(b))
-        for ch in range(channels):
-            for h in range(high_count):
-                for o in range(low_count):
-                    start = (h * low_count + o) * slab
-                    value = light[b, ch, margin + start : margin + start + slab, :]
-                    if start < margin:
-                        value = value + light_above[b, ch, start : start + slab, :]
-                    if start >= strip - margin:
-                        start = start - (strip - margin)
-                        value = value + light_below[b, ch, start : start + slab, :]
-                    middle[b, o, h, ch] = value
-        for d in range(1, low_count):
-            to_low(b, d).start()
+        send_slabs(b, outer, (1, 2))
+        sum_slabs(b, inner, (0,))
 
     @pl.when(jnp.logical_and(step >= 2, step < blocks + 2))
     def _():
-        b = step - 2
-        for d in range(1, low_count):
-            to_low(b, d).wait()
-        total = middle[b, low]
-        for d in range(1, low_count):
-            total = total + got_low[b, d - 1]
-        part[b] = total
-        for d in range(1, high_count):
-            to_high(b, d).start()
+        sum_slabs(step - 2, outer, (1, 2))
 
     @pl.when(step >= 3)
     def _():
@@ -441,11 +469,12 @@
             vmem,
             vmem,
             pl.BlockSpec((waves, strip, side), lambda s: (0, 0, jnp.minimum(s, tile_cols - 1))),
-            vmem,
+            pl.BlockSpec(memory_space=pl.ANY),
         ],
         out_specs=vmem,
         out_shape=jax.ShapeDtypeStruct((channels, slab, tile_cols * side), f32),
         scratch_shapes=[
+            pltpu.VMEM(bank.shape, f32),
             pltpu.VMEM((tile_cols, waves, side, side), f32),
             pltpu.VMEM((tile_cols, waves, side, side), f32),
             pltpu.VMEM((planes * length, side), f32),
@@ -461,12 +490,13 @@
             pltpu.VMEM((blocks, low_count - 1, high_count, channels, slab, side), f32),
             pltpu.VMEM((blocks, high_count, channels, slab, side), f32),
             pltpu.VMEM((blocks, high_count - 1, channels, slab, side), f32),
+            sems((tile_cols,)),
             sems((2, tile_cols)),
             sems((2, tile_cols)),
             sems((2, blocks)),
             sems((2, blocks)),
-            sems((blocks, low_count - 1)),
-            sems((blocks, low_count - 1)),
+            sems((blocks, low_count - 1, 3)),
+            sems((blocks, low_count - 1, 3)),
             sems((blocks, high_count - 1)),
             sems((blocks, high_count - 1)),
         ],

time: 78.6 us -> 73.9 us (0.940)
  the two profiles are of different devices: /device:TPU:4 before, /device:TPU:0 now
where the time goes in v6:
time: 73.9 us; the launch traced here: 73.8 us
  Pallas kernels  72 us (97%)
  local copies, waits for them, and re-layouts  1.77 us (2%)
    pallas_call x1, Pallas kernels, camera(): pl.pallas_call(functools.partial(camera_kernel, dims), grid=(blocks + 3,)...  72 us
    unnamed x1, local copies, waits for them, and re-layouts  1.77 us

profile of v6, /device:TPU:0, one launch (start us, length us, event | category | flops | bytes accessed | tf_op | source)
XLA Modules:
  0.0 73.8 jit_solution(1984573020890680259)
XLA Ops:
  0.0 72.0 %camera.1 = f32[3,32,1024]{2,1,0:T(8,128)} custom-call(s32[2,4,8]{2,1,0:T(4,128)} %bitcast.2, s32[2,4,8]{2,1,0:T(4,128)} %bitcast.3, f32[3,32]{1,0:T(4,128)} %response_ref.1, bf16[256,384]{1,0:T(8,128)(2,1)} %constant.8.clone.rows_in, bf16[384,256]{1,0:T(8,128)(2,1)} %constant.9.clone.cols_in, bf16[768,256]{1,0:T(8,128)(2,1)} %constant.10.clone.cols_out, ...), custom_call_target="tpu_custom_call" | custom-call | flops 13690208256 | bytes 8388608 | tf_op jit(solution)/shard_map/camera/pallas_call | solution.py:460
  72.0 1.8 %copy.11 = f32[3,32,1024]{2,1,0:T(8,128)} copy(f32[3,32,1024]{2,1,0:T(8,128)} %camera.1) | data formatting | bytes 786432

commit v7 on v6

--- a/solution.py
+++ b/solution.py
@@ -22,6 +22,12 @@
 def left_factor(table):
     high, low = halves(table)
     return np.concatenate([high, high, low], axis=1)
+
+
+def stacked_factor(table):
+    high, low = halves(table)
+    top = np.concatenate([high, high], axis=1)
+    return np.concatenate([top, np.concatenate([low, np.zeros_like(low)], axis=1)], axis=0)
 
 
 def right_factor(table):
@@ -38,7 +44,7 @@
     cols_in = np.concatenate([cosine[:, :side].T, sine[:, :side].T], axis=1)
     cols_out = np.concatenate([cosine, sine], axis=0)
     rows_out = np.concatenate([cosine.T, -sine.T], axis=1) * (2.0 / (length * length))
-    return left_factor(rows_in), right_factor(cols_in), right_factor(cols_out), left_factor(rows_out)
+    return stacked_factor(rows_in), right_factor(cols_in), right_factor(cols_out), left_factor(rows_out)
 
 
 def split(values):
@@ -56,11 +62,6 @@
     out_ref[0:side, lanes] = high
     out_ref[side : 2 * side, lanes] = low
     out_ref[2 * side : 3 * side, lanes] = high
-
-
-def lift(values):
-    high, low = split(values)
-    return [high, low, high]
 
 
 def camera_kernel(
@@ -272,8 +273,9 @@
             light_below[...] = jnp.zeros_like(light_below)
 
     def transform_rows(mid, fields, t):
-        pair = [jnp.concatenate(lift(field), axis=0) for field in (fields(t), fields(t + 1))]
+        pair = [jnp.concatenate(split(field), axis=0) for field in (fields(t), fields(t + 1))]
         first = dot(rows_in[...], jnp.concatenate(pair, axis=1))
+        first = first[:length] + first[length:]
         for j in range(2):
             upper_bits, lower_bits = split(first[:, j * side : (j + 1) * side])
             rows = slice((t + j) * length, (t + j + 1) * length)

time: 73.9 us -> 73.9 us (level)
  no operation moved by 1% of the time
where the time goes in v7:
time: 73.9 us; the launch traced here: 73.7 us
  Pallas kernels  72 us (97%)
  local copies, waits for them, and re-layouts  1.77 us (2%)
    pallas_call x1, Pallas kernels, camera(): pl.pallas_call(functools.partial(camera_kernel, dims), grid=(blocks + 3,)...  72 us
    unnamed x1, local copies, waits for them, and re-layouts  1.77 us

profile of v7, /device:TPU:0, one launch (start us, length us, event | category | flops | bytes accessed | tf_op | source)
XLA Modules:
  0.0 73.7 jit_solution(1083683611902221177)
XLA Ops:
  0.0 72.0 %camera.1 = f32[3,32,1024]{2,1,0:T(8,128)} custom-call(s32[2,4,8]{2,1,0:T(4,128)} %bitcast.2, s32[2,4,8]{2,1,0:T(4,128)} %bitcast.3, f32[3,32]{1,0:T(4,128)} %response_ref.1, bf16[512,256]{1,0:T(8,128)(2,1)} %constant.8.clone.rows_in, bf16[384,256]{1,0:T(8,128)(2,1)} %constant.9.clone.cols_in, bf16[768,256]{1,0:T(8,128)(2,1)} %constant.10.clone.cols_out, ...), custom_call_target="tpu_custom_call" | custom-call | flops 13690208256 | bytes 8388608 | tf_op jit(solution)/shard_map/camera/pallas_call | solution.py:462
  72.0 1.8 %copy.11 = f32[3,32,1024]{2,1,0:T(8,128)} copy(f32[3,32,1024]{2,1,0:T(8,128)} %camera.1) | data formatting | bytes 786432
